TPU v7x, 32 devices: a whole 2x2x4 slice. The times are simulated.
32 devices in a mesh: head: 2 (over core), seq: 16 (over z, y, x).
Axes of the slice: x: 2, y: 2, z: 4, core: 2. Of those that a mesh axis runs over, the one named last changes fastest.
Arguments:
- inputs: bfloat16 [2, 4096, 1152], P('head', 'seq'), may hold values from -6 to 6
- cotangent: bfloat16 [2, 4096, 1152], P('head', 'seq'), may hold values from -6 to 6
- teacher: bfloat16 [2, 4096, 1152], P('head', 'seq'), may hold values from -6 to 6
- segments: int32 [2, 4096], replicated, may hold values from 0 to 3, as said below
- valid_mask: int32 [2, 4096], P('head', 'seq'), may hold values from 0 to 1, as said below
- w_qkv: float32 [2, 1152, 1536], P(None, 'seq', 'head'), may hold values from -0.1875 to 0.1875
- w_out: float32 [2, 1024, 1152], P(None, 'seq', 'head'), may hold values from -0.1875 to 0.1875
- w_gu: float32 [2, 1152, 13824], P(None, 'seq', 'head'), may hold values from -0.1875 to 0.1875
- w_down: float32 [2, 6912, 1152], P(None, 'seq', 'head'), may hold values from -0.078125 to 0.078125
- norm_gains: float32 [2, 2, 2560], P(None, 'head', 'seq'), may hold values from 0.5 to 1.5
- mom_qkv: float32 [2, 1152, 1536], P(None, 'seq', 'head')
- mom_out: float32 [2, 1024, 1152], P(None, 'seq', 'head')
- mom_gu: float32 [2, 1152, 13824], P(None, 'seq', 'head')
- mom_down: float32 [2, 6912, 1152], P(None, 'seq', 'head')
- gain_first: float32 [2, 2, 2560], P(None, 'head', 'seq'), may hold values from -2275.5556 to 2275.5556
- gain_second: float32 [2, 2, 2560], P(None, 'head', 'seq'), may hold values from 431.1579 to 3532045.5
Outputs:
- mse_loss: float32 [], replicated
- layer_output: float32 [2, 4096, 1152], P('head', 'seq')
- input_grad: float32 [2, 4096, 1152], P('head', 'seq')
- qkv_new: float32 [2, 1152, 1536], P(None, 'seq', 'head')
- out_new: float32 [2, 1024, 1152], P(None, 'seq', 'head')
- gate_up_new: float32 [2, 1152, 13824], P(None, 'seq', 'head')
- down_new: float32 [2, 6912, 1152], P(None, 'seq', 'head')
- qkv_moment: float32 [2, 1152, 1536], P(None, 'seq', 'head')
- out_moment: float32 [2, 1024, 1152], P(None, 'seq', 'head')
- gate_up_moment: float32 [2, 1152, 13824], P(None, 'seq', 'head')
- down_moment: float32 [2, 6912, 1152], P(None, 'seq', 'head')
- gains_new: float32 [2, 2, 2560], P(None, 'head', 'seq')
- gain_first_new: float32 [2, 2, 2560], P(None, 'head', 'seq')
- gain_second_new: float32 [2, 2, 2560], P(None, 'head', 'seq')
Inputs may be any that keep to these rules, and one draw needn't show every extreme that they name: `segments`: along each sequence the ids start at 0 and never fall; a document is a run of equal ids. In every draw one sequence is one document from end to end, and every other sequence holds exactly four documents, ids 0 to 3. `valid_mask`: the last position of every sequence is valid.
All inputs are finite; a program needn't handle non-finite values.
Results may differ from a plain program's by a relative error of at most 0.02.
The roundings to bfloat16 on the way count: a program that leaves them out, or rounds other values in their place, can miss the bound.
Values may be sent and summed in bfloat16 or wider, within the bound.
A program may use at most 512 MiB of HBM per device.

v0:
```python
from functools import partial
import itertools
import math

import jax
import jax.numpy as jnp
from jax import lax
from jax.experimental import pallas as pl
from jax.experimental.pallas import tpu as pltpu
from jax.sharding import Mesh, PartitionSpec as P

D = 1152
HEADS = 4
HD = 256
FF = 6912
WINDOW = 512
LAYERS = 2
NS_ITERS = 5
STEP = 10
PLANE = 4

norm_eps = 1e-06
rope_base = 10000.0
newton_one = 3.4445
newton_two = -4.775
newton_three = 2.0315
muon_decay = 0.95
muon_rate = 0.15
muon_shrink = 0.01
muon_scale = 0.2
beta_one = 0.9
beta_two = 0.95
adam_rate = 0.7
adam_epsilon = 1e-08
finest_precision = lax.Precision.HIGHEST
MESH = pl.DeviceIdType.MESH
SEQ = ("zd", "tp")
GROUP = ("head", "tp")
EVERY = ("head", "zd", "tp")
bf16 = jnp.bfloat16
f32 = jnp.float32
LIGHT = pl.CostEstimate(flops=1, bytes_accessed=1, transcendentals=0)


def linear(places, sizes):
    index = 0
    for place, size in zip(places, sizes):
        index = index * size + place
    return index


def enter(partners):
    barrier = pltpu.get_barrier_semaphore()
    for partner in partners:
        pl.semaphore_signal(barrier, inc=1, device_id=partner, device_id_type=MESH)
    pl.semaphore_wait(barrier, len(partners))


class Spread:
    ORDER = ("zd", "tp", "head")

    def __init__(self, sizes, slots, send_sem, recv_sem, whole_z=False):
        self.size = dict(zip(EVERY, sizes))
        self.place = {axis: lax.axis_index(axis) for axis in EVERY}
        self.slots, self.send_sem, self.recv_sem = slots, send_sem, recv_sem
        self.held, self.sends, self.number = [(self.place, None)], [], 0
        if whole_z:
            self.held = [(dict(self.place, zd=z), None) for z in range(self.size["zd"])]
            self.ORDER = self.ORDER[1:]

    def partners(self):
        return [
            {axis: lax.rem(self.place[axis] + step, self.size[axis])}
            for axis in self.ORDER
            for step in range(1, self.size[axis])
        ]

    def stage(self, axis):
        arriving = []
        for where, arrivals in self.held:
            while arrivals:
                arrivals.pop().wait_recv()
            for step in range(1, self.size[axis]):
                to = lax.rem(self.place[axis] + step, self.size[axis])
                back = lax.rem(self.place[axis] - step + self.size[axis], self.size[axis])
                landing = []
                for k, slot in enumerate(self.slots):
                    ref = slot.at[tuple(where[name] for name in EVERY)]
                    copy = pltpu.make_async_remote_copy(
                        src_ref=ref,
                        dst_ref=ref,
                        send_sem=self.send_sem.at[k, self.number],
                        recv_sem=self.recv_sem.at[k, self.number],
                        device_id={axis: to},
                        device_id_type=MESH,
                    )
                    copy.start()
                    self.sends.append(copy)
                    landing.append(copy)
                self.number += 1
                arriving.append((dict(where, **{axis: back}), landing))
        self.held = self.held + arriving

    def finish(self):
        for _, arrivals in self.held:
            while arrivals:
                arrivals.pop().wait_recv()
        for copy in self.sends:
            copy.wait_send()


def start_kernel(sizes, *refs):
    cores, planes, members = sizes
    rest = list(refs)
    take = lambda number: [rest.pop(0) for _ in range(number)]
    gu, qkv, out, packet = take(4)
    gu_result, mixed, project, packets, qkv_later, out_later = take(6)
    packet_slots, qkv_slots, out_slots, send_sem, recv_sem = take(5)
    pieces, gu_send, gu_recv, gu_own, later_send, later_recv = take(6)
    qkv_low, out_low, later_own = take(3)
    gather = Spread(sizes, [packet_slots, qkv_slots, out_slots], send_sem, recv_sem)
    here = tuple(gather.place[name] for name in EVERY)
    core, zd, tp = here
    group = []
    for step in range(1, cores * members):
        far = lax.rem(core + step // members, cores), lax.rem(tp + step % members, members)
        group.append((dict(zip(GROUP, far)), linear(far, (cores, members))))
    enter(gather.partners() + [device for device, _ in group])
    packet_slots[here] = packet[...]

    def place_rows(source, layer, slot, index):
        rows = source.shape[1]
        slot[index + (slice(0, rows),)] = source[layer].astype(bf16)
        if slot.shape[-2] > rows:
            slot[index + (slice(rows, slot.shape[-2]),)] = jnp.zeros(
                (slot.shape[-2] - rows, slot.shape[-1]), bf16
            )

    for source, slot in ((qkv, qkv_slots), (out, out_slots)):
        place_rows(source, 0, slot, here)
    gather.stage("zd")
    moves = []

    def along_z(source, target, sends, recvs):
        for step in range(1, planes):
            copy = pltpu.make_async_remote_copy(
                src_ref=source,
                dst_ref=target,
                send_sem=sends.at[step],
                recv_sem=recvs.at[step],
                device_id={"zd": lax.rem(zd + step, planes)},
                device_id_type=MESH,
            )
            copy.start()
            moves.append(copy)

    for k, (source, low, slot) in enumerate(
        ((qkv, qkv_low, qkv_later), (out, out_low, out_later))
    ):
        for layer in range(1, source.shape[0]):
            place_rows(source, layer, low, (layer - 1,))
            target = slot.at[layer - 1, zd]
            along_z(
                low.at[layer - 1], target, later_send.at[k, layer], later_recv.at[k, layer]
            )
            own = pltpu.make_async_copy(low.at[layer - 1], target, later_own.at[k, layer])
            own.start()
            moves.append(own)
    layers, rows, columns = gu.shape
    block = columns // (planes * members)
    half = planes // cores
    for c in range(cores):
        for j in range(members):
            for i in range(layers):
                cut = [
                    gu[i, :, pl.ds(((c * half + k) * members + j) * block, block)]
                    for k in range(half)
                ]
                value = jnp.concatenate(cut, axis=1) if half > 1 else cut[0]
                pieces[c * members + j, i * rows : (i + 1) * rows] = value.astype(bf16)
    if pieces.shape[1] > layers * rows:
        for piece in range(cores * members):
            pieces[piece, layers * rows :] = jnp.zeros(
                (pieces.shape[1] - layers * rows, pieces.shape[2]), bf16
            )
    me = linear((core, tp), (cores, members))
    for step, (device, index) in enumerate(group):
        copy = pltpu.make_async_remote_copy(
            src_ref=pieces.at[index],
            dst_ref=gu_result.at[me],
            send_sem=gu_send.at[step],
            recv_sem=gu_recv.at[step],
            device_id=device,
            device_id_type=MESH,
        )
        copy.start()
        moves.append(copy)
    own = pltpu.make_async_copy(pieces.at[me], gu_result.at[me], gu_own)
    own.start()
    moves.append(own)
    gather.stage("tp")
    gather.stage("head")
    gather.finish()
    side_by_side(sizes, (qkv_slots, out_slots), (mixed, project))
    packets[...] = packet_slots[...]
    for copy in moves:
        copy.wait()


def side_by_side(sizes, slots, results):
    cores, planes, members = sizes
    for slot, result in zip(slots, results):
        columns = slot.shape[4]
        rows = result.shape[0] // (planes * members)
        for h, z, t in itertools.product(range(cores), range(planes), range(members)):
            row = (z * members + t) * rows
            result[row : row + rows, h * columns : (h + 1) * columns] = slot[h, z, t, :rows]


def later_kernel(sizes, layer, qkv, out, mixed, project, qkv_slots, out_slots, send_sem, recv_sem):
    gather = Spread(sizes, [qkv_slots, out_slots], send_sem, recv_sem, whole_z=True)
    core, _, tp = (gather.place[name] for name in EVERY)
    enter(gather.partners())
    for source, slot in ((qkv, qkv_slots), (out, out_slots)):
        for z in range(sizes[1]):
            slot[core, z, tp] = source[layer - 1, z]
    gather.stage("tp")
    gather.stage("head")
    gather.finish()
    side_by_side(sizes, (qkv_slots, out_slots), (mixed, project))


def whole_shapes(sizes, tall, matrices):
    slots = [pltpu.VMEM(sizes + (t, w.shape[2]), bf16) for t, w in zip(tall, matrices)]
    outs = [
        jax.ShapeDtypeStruct((w.shape[1] * sizes[1] * sizes[2], w.shape[2] * sizes[0]), bf16)
        for w in matrices
    ]
    return slots, outs


def start(w_gu, w_qkv, w_out, packet, ident):
    sizes = tuple(lax.axis_size(axis) for axis in EVERY)
    cores, planes, members = sizes
    vmem, dma = pltpu.VMEM, pltpu.SemaphoreType.DMA
    here, there = pl.BlockSpec(memory_space=pltpu.VMEM), pl.BlockSpec(memory_space=pl.ANY)
    shape = jax.ShapeDtypeStruct
    tall = [-(-w.shape[1] // 16) * 16 for w in (w_qkv, w_out)]
    slots, outs = whole_shapes(sizes, tall, (w_qkv, w_out))
    layers, rows, columns = w_gu.shape
    piece = (
        cores * members,
        -(-layers * rows // 16) * 16,
        columns // (cores * members),
    )
    later = [
        shape((layers - 1, planes, t, w.shape[2]), bf16) for t, w in zip(tall, (w_qkv, w_out))
    ]
    operands = [w_gu, w_qkv, w_out, packet]
    outs = [shape(piece, bf16)] + outs + [shape(sizes + packet.shape, f32)] + later
    out_specs = [there] + [here] * 3 + [there] * 2
    moves = math.prod(sizes) - 1
    scratch = [vmem(sizes + packet.shape, f32)] + slots + [dma((3, moves))] * 2
    scratch += [vmem(piece, bf16), dma((cores * members - 1,)), dma((cores * members - 1,)), dma]
    scratch += [dma((2, layers, planes))] * 2
    scratch += [
        vmem((layers - 1, t, w.shape[2]), bf16) for t, w in zip(tall, (w_qkv, w_out))
    ] + [dma((2, layers))]
    return pl.pallas_call(
        partial(start_kernel, sizes),
        out_shape=outs,
        in_specs=[here] * len(operands),
        out_specs=out_specs,
        scratch_shapes=scratch,
        compiler_params=pltpu.CompilerParams(
            collective_id=ident, has_side_effects=True, vmem_limit_bytes=56 * 2**20
        ),
    )(*operands)


def later_weights(gathered, w_qkv, w_out, layer, ident):
    sizes = tuple(lax.axis_size(axis) for axis in EVERY)
    slots, outs = whole_shapes(sizes, [g.shape[2] for g in gathered], (w_qkv, w_out))
    here = pl.BlockSpec(memory_space=pltpu.VMEM)
    moves = math.prod(sizes) - sizes[1]
    return pl.pallas_call(
        partial(later_kernel, sizes, layer),
        out_shape=outs,
        in_specs=[here] * 2,
        out_specs=[here] * 2,
        scratch_shapes=slots + [pltpu.SemaphoreType.DMA((2, moves))] * 2,
        compiler_params=pltpu.CompilerParams(
            collective_id=ident, has_side_effects=True, vmem_limit_bytes=48 * 2**20
        ),
    )(*gathered)


def by_rows(rows, work, step=16):
    @pl.loop(0, rows // step)
    def _(index):
        work(pl.ds(pl.multiple_of(index * step, step), step))


def collect_kernel(sizes, layers, tiled, *refs):
    cores, planes, members = sizes
    rest = list(refs)
    take = lambda number: [rest.pop(0) for _ in range(number)]
    acts, packet = take(4 * layers), take(1)[0]
    if tiled:
        (down,) = take(1)
    results = take(3)
    if tiled:
        (down_result,) = take(1)
    far, halves = take(4 * layers), take(2 * layers)
    packet_land = rest.pop(0)
    pieces, plane_lands, totals, z_sums, z_lands = (take(3) for _ in range(5))
    act_send, act_recv, packet_send, packet_recv = take(4)
    tp_send, tp_recv, z_send, z_recv = take(4)
    core, zd, tp = (lax.axis_index(axis) for axis in EVERY)
    sibling = {"head": 1 - core}
    enter(
        [sibling]
        + [{"tp": lax.rem(tp + step, members)} for step in range(1, members)]
        + [{"zd": lax.rem(zd + step, planes)} for step in range(1, planes)]
    )
    sends = []

    def send(src, dst, send_sem, recv_sem, device):
        copy = pltpu.make_async_remote_copy(
            src_ref=src,
            dst_ref=dst,
            send_sem=send_sem,
            recv_sem=recv_sem,
            device_id=device,
            device_id_type=MESH,
        )
        copy.start()
        sends.append(copy)
        return copy

    if tiled:
        down_land, down_send, down_recv, down_own = take(4)
        down_moves = []
        for step in range(1, planes):
            there = lax.rem(zd + step, planes)
            down_moves.append(
                send(
                    down.at[there],
                    down_land.at[step],
                    down_send.at[step],
                    down_recv.at[step],
                    {"zd": there},
                )
            )
        down_stay = pltpu.make_async_copy(down.at[zd], down_land.at[0], down_own)
        down_stay.start()
    for k in range(2 * layers):
        grad, half = acts[2 * k + 1], halves[k]
        width = half.shape[2]
        for h in range(cores):
            half[h] = grad[:, h * width : (h + 1) * width]
    moves = []
    for k in range(2 * layers):
        moves.append(
            send(acts[2 * k], far[2 * k], act_send.at[2 * k], act_recv.at[2 * k], sibling)
        )
        moves.append(
            send(
                halves[k].at[1 - core],
                far[2 * k + 1],
                act_send.at[2 * k + 1],
                act_recv.at[2 * k + 1],
                sibling,
            )
        )
    gains = send(packet.at[1 - core], packet_land, packet_send, packet_recv, sibling)
    plane_moves, z_moves = {}, {}
    for kind in range(3):
        piece = pieces[kind]
        if kind < 2:
            for layer in range(layers):
                k = 2 * layer + kind
                near = lax.dot_general(
                    acts[2 * k][...], halves[k][core], ALONG, preferred_element_type=f32
                )
                moves[2 * k].wait_recv()
                moves[2 * k + 1].wait_recv()
                value = near + lax.dot_general(
                    far[2 * k][...], far[2 * k + 1][...], ALONG, preferred_element_type=f32
                )
                value = value.astype(bf16)
                rows = value.shape[0] // (planes * members)
                slab = piece.shape[1] // planes
                for z, t in itertools.product(range(planes), range(members)):
                    at = (z * members + t) * rows
                    to = z * slab + layer * rows
                    piece[t, to : to + rows] = value[at : at + rows]
            if slab > layers * rows:
                for z, t in itertools.product(range(planes), range(members)):
                    piece[t, z * slab + layers * rows : (z + 1) * slab] = jnp.zeros(
                        (slab - layers * rows, piece.shape[2]), bf16
                    )
        else:
            gains.wait_recv()
            piece[...] = packet[core] + packet_land[...]
        for step in range(1, members):
            there = lax.rem(tp + step, members)
            plane_moves[kind, step] = send(
                piece.at[there],
                plane_lands[kind].at[step],
                tp_send.at[kind, step],
                tp_recv.at[kind, step],
                {"tp": there},
            )
    for kind in range(3):
        for step in range(1, members):
            plane_moves[kind, step].wait_recv()
        piece, total, land, result = pieces[kind], totals[kind], plane_lands[kind], results[kind]
        stride = 8 if land.dtype == f32 else 16

        def gather_plane(rows):
            value = piece[tp, rows].astype(f32)
            for step in range(1, members):
                value = value + land[step, rows].astype(f32)
            total[rows] = value

        by_rows(total.shape[0], gather_plane, stride)
        height = result.shape[0]
        z_sum = z_sums[kind]
        for step in range(1, planes):
            there = lax.rem(zd + step, planes)

            def round_off(rows):
                at = pl.multiple_of(there * height + rows.start, stride)
                z_sum[step, rows] = total[pl.ds(at, rows.size)].astype(z_sum.dtype)

            by_rows(height, round_off, stride)
            z_moves[kind, step] = send(
                z_sum.at[step],
                z_lands[kind].at[step],
                z_send.at[kind, step],
                z_recv.at[kind, step],
                {"zd": there},
            )
    for kind in range(3):
        for step in range(1, planes):
            z_moves[kind, step].wait_recv()
        total, land, result = totals[kind], z_lands[kind], results[kind]
        height = result.shape[0]
        stride = 8 if land.dtype == f32 else 16

        def gather_z(rows):
            at = pl.multiple_of(zd * height + rows.start, stride)
            value = total[pl.ds(at, rows.size)]
            for step in range(1, planes):
                value = value + land[step, rows].astype(f32)
            result[rows] = value

        by_rows(height, gather_z, stride)
    if tiled:
        down_stay.wait()
        for copy in down_moves:
            copy.wait_recv()

        def gather_down(rows):
            value = down_land[0, rows].astype(f32)
            for step in range(1, planes):
                value = value + down_land[step, rows].astype(f32)
            down_result[rows] = value

        by_rows(down_result.shape[0], gather_down)
    for copy in sends:
        copy.wait_send()


def collect(acts, packet, down, ident):
    sizes = tuple(lax.axis_size(axis) for axis in EVERY)
    cores, planes, members = sizes
    layers = len(acts) // 4
    vmem, dma = pltpu.VMEM, pltpu.SemaphoreType.DMA
    tokens = acts[0].shape[0]
    halves = [acts[2 * k + 1].shape[1] // cores for k in range(2 * layers)]
    slabs = []
    for kind in range(2):
        rows = layers * acts[2 * kind].shape[1] // (planes * members)
        slabs.append((-(-rows // 16) * 16, halves[kind], bf16))
    slabs.append((packet.shape[2] // planes, packet.shape[3], f32))
    far = []
    for k in range(2 * layers):
        far += [vmem(acts[2 * k].shape, bf16), vmem((tokens, halves[k]), bf16)]
    scratch = far + [vmem((cores, tokens, width), bf16) for width in halves]
    scratch += [vmem(packet.shape[1:], f32)]
    scratch += [vmem((members, planes * r, c), kind) for r, c, kind in slabs] * 2
    scratch += [vmem((planes * r, c), f32) for r, c, _ in slabs]
    scratch += [vmem((planes, r, c), kind) for r, c, kind in slabs] * 2
    scratch += [dma((4 * layers,))] * 2 + [dma] * 2
    scratch += [dma((3, members))] * 2 + [dma((3, planes))] * 2
    here = pl.BlockSpec(memory_space=pltpu.VMEM)
    operands = [*acts, packet]
    outs = [jax.ShapeDtypeStruct((r, c), f32) for r, c, _ in slabs]
    in_specs = [here] * len(operands)
    if down is not None:
        operands, in_specs = operands + [down], in_specs + [pl.BlockSpec(memory_space=pl.ANY)]
        outs += [jax.ShapeDtypeStruct(down.shape[1:], f32)]
        scratch += [vmem(down.shape, bf16), dma((planes,)), dma((planes,)), dma]
    return pl.pallas_call(
        partial(collect_kernel, sizes, layers, down is not None),
        out_shape=outs,
        in_specs=in_specs,
        out_specs=[here] * len(outs),
        scratch_shapes=scratch,
        cost_estimate=LIGHT,
        compiler_params=pltpu.CompilerParams(
            collective_id=ident, has_side_effects=True, vmem_limit_bytes=56 * 2**20
        ),
    )(*operands)


def neighbours(planes, reach, sign):
    total = planes * PLANE
    place = linear([lax.axis_index("zd"), lax.axis_index("tp")], (planes, PLANE))

    def at(distance):
        there = lax.rem(place + distance + total, total)
        return {"zd": lax.div(there, PLANE), "tp": lax.rem(there, PLANE)}

    steps = range(1, reach + 1)
    return [at(sign * step) for step in steps], [at(-sign * step) for step in steps]


def inverse_rms(values):
    return lax.rsqrt(jnp.mean(values * values, axis=-1, keepdims=True) + norm_eps)


def rms_back(gradient, values, gain):
    inverse = inverse_rms(values)
    scaled = gradient * gain
    shared = jnp.mean(scaled * values, axis=-1, keepdims=True) * (inverse * inverse)
    return inverse * (scaled - values * shared), jnp.sum(
        gradient * values * inverse, axis=0, keepdims=True
    )


def turn(values, cosine, sine):
    half = values.shape[-1] // 2
    lower, upper = values[:, :half], values[:, half:]
    return jnp.concatenate(
        [lower * cosine - upper * sine, upper * cosine + lower * sine], axis=-1
    )


def soft_rows(query, keys, bias):
    scores = lax.dot_general(query, keys, ACROSS, preferred_element_type=f32)
    scores = scores * (1.0 / math.sqrt(HD)) + bias
    raised = jnp.exp(scores - jnp.max(scores, axis=-1, keepdims=True))
    return raised / jnp.sum(raised, axis=-1, keepdims=True)


def attn_forward_kernel(planes, reach, chained, *refs):
    rest = list(refs)
    take = lambda number: [rest.pop(0) for _ in range(number)]
    if chained:
        base, down, before = take(3)
    else:
        (base,) = take(1)
    w_mixed, w_project, gains, cosine, sine, bias = take(6)
    hidden, normed, mixed, queries, keyvals_out = take(5)
    attended, projected, hidden_half, normed_ffn = take(4)
    keyvals, send_sem, recv_sem, save_sem = take(4)
    seqs, stretch, key_len = bias.shape
    devices, sources = neighbours(planes, reach, 1)
    enter(devices + sources)
    value = base[...].astype(f32)
    if chained:
        late = down[...]
        value = value + late * inverse_rms(late) * before[1:2, D : 2 * D]
    hidden[...] = value
    low = (value * inverse_rms(value) * gains[0:1, :D]).astype(bf16)
    normed[...] = low
    mixed[...] = matmul(low, w_mixed[...])
    key = mixed[:, HEADS * HD : HEADS * HD + HD]
    key = turn(key * inverse_rms(key) * gains[1:2, 2 * D :], cosine[...], sine[...]).astype(bf16)
    late_values = mixed[:, HEADS * HD + HD :].astype(bf16)
    copies = []
    for i in range(seqs):
        rows = slice(i * stretch, (i + 1) * stretch)
        keyvals[i, reach * stretch :, :HD] = key[rows]
        keyvals[i, reach * stretch :, HD:] = late_values[rows]
        for step, device in enumerate(devices):
            copy = pltpu.make_async_remote_copy(
                src_ref=keyvals.at[i, pl.ds(reach * stretch, stretch)],
                dst_ref=keyvals.at[i, pl.ds((reach - 1 - step) * stretch, stretch)],
                send_sem=send_sem.at[i, step],
                recv_sem=recv_sem.at[i, step],
                device_id=device,
                device_id_type=MESH,
            )
            copy.start()
            copies.append(copy)
    for h in range(HEADS):
        columns = slice(h * HD, (h + 1) * HD)
        query = mixed[:, columns]
        query = turn(query * inverse_rms(query) * gains[0:1, 2 * D :], cosine[...], sine[...])
        queries[:, columns] = query.astype(bf16)
    for copy in copies:
        copy.wait_recv()
    save = pltpu.make_async_copy(keyvals, keyvals_out, save_sem)
    save.start()
    for i in range(seqs):
        rows = slice(i * stretch, (i + 1) * stretch)
        for h in range(HEADS):
            columns = slice(h * HD, (h + 1) * HD)
            soft = soft_rows(queries[rows, columns], keyvals[i, :, :HD], bias[i])
            attended[rows, columns] = matmul(soft.astype(bf16), keyvals[i, :, HD:]).astype(bf16)
    out = matmul(attended[...], w_project[...])
    projected[...] = out
    half = hidden[...] + out * inverse_rms(out) * gains[0:1, D : 2 * D]
    hidden_half[...] = half
    normed_ffn[...] = (half * inverse_rms(half) * gains[1:2, :D]).astype(bf16)
    for copy in copies:
        copy.wait_send()
    save.wait()


def attn_forward(base, weights, gains, tables, bias, planes, reach, ident, earlier=None):
    tokens = base.shape[0]
    seqs, _, key_len = bias.shape
    shape = jax.ShapeDtypeStruct
    operands = [base] + list(earlier or []) + list(weights) + [gains, *tables, bias]
    here, there = pl.BlockSpec(memory_space=pltpu.VMEM), pl.BlockSpec(memory_space=pl.ANY)
    dma = pltpu.SemaphoreType.DMA
    return pl.pallas_call(
        partial(attn_forward_kernel, planes, reach, earlier is not None),
        out_shape=[
            shape((tokens, D), f32),
            shape((tokens, D), bf16),
            shape((tokens, weights[0].shape[1]), f32),
            shape((tokens, HEADS * HD), bf16),
            shape((seqs, key_len, 2 * HD), bf16),
            shape((tokens, HEADS * HD), bf16),
            shape((tokens, D), f32),
            shape((tokens, D), f32),
            shape((tokens, D), bf16),
        ],
        in_specs=[here] * len(operands),
        out_specs=[here] * 4 + [there] + [here] * 4,
        scratch_shapes=[
            pltpu.VMEM((seqs, key_len, 2 * HD), bf16),
            dma((seqs, reach)),
            dma((seqs, reach)),
            dma,
        ],
        compiler_params=pltpu.CompilerParams(
            collective_id=ident, has_side_effects=True, vmem_limit_bytes=56 * 2**20
        ),
    )(*operands)


def attn_backward_kernel(planes, reach, chained, *refs):
    rest = list(refs)
    take = lambda number: [rest.pop(0) for _ in range(number)]
    d_ffn, above, hidden, mixed, queries, keyvals, projected, hidden_half = take(8)
    w_mixed, w_project, gains, cosine, sine, bias = take(6)
    if chained:
        down, before = take(2)
    grad, d_mixed, d_projected, gain_grads = take(4)
    if chained:
        d_down, d_post = take(2)
    d_keyvals, outgoing, incoming, d_attended, send_sem, recv_sem = take(6)
    seqs, stretch, key_len = bias.shape
    devices, sources = neighbours(planes, reach, -1)
    enter(devices + sources)
    scale = 1.0 / math.sqrt(HD)
    part, gain_row = rms_back(d_ffn[...], hidden_half[...], gains[1:2, :D])
    gain_grads[1:2, :D] = gain_row
    gain_grads[1:2, D : 2 * D] = jnp.zeros((1, D), f32)
    grad[...] = part + above[...]
    part, gain_row = rms_back(grad[...], projected[...], gains[0:1, D : 2 * D])
    gain_grads[0:1, D : 2 * D] = gain_row
    low = part.astype(bf16)
    d_projected[...] = low
    d_attended[...] = lax.dot_general(
        low, w_project[...], ACROSS, preferred_element_type=f32
    ).astype(bf16)
    query_gain = jnp.zeros((1, HD), f32)
    for i in range(seqs):
        rows = slice(i * stretch, (i + 1) * stretch)
        d_keys = d_values = None
        for h in range(HEADS):
            columns = slice(h * HD, (h + 1) * HD)
            query, d_out = queries[rows, columns], d_attended[rows, columns]
            keys, values = keyvals[i, :, :HD], keyvals[i, :, HD:]
            soft = soft_rows(query, keys, bias[i])
            d_soft = lax.dot_general(d_out, values, ACROSS, preferred_element_type=f32)
            total = jnp.sum(soft * d_soft, axis=-1, keepdims=True)
            d_scores = (soft * (d_soft - total)).astype(bf16)
            key_part = lax.dot_general(d_scores, query, ALONG, preferred_element_type=f32)
            value_part = lax.dot_general(
                soft.astype(bf16), d_out, ALONG, preferred_element_type=f32
            )
            d_keys = key_part if d_keys is None else d_keys + key_part
            d_values = value_part if d_values is None else d_values + value_part
            d_query = matmul(d_scores, keys) * scale
            d_query = turn(d_query, cosine[rows], -sine[rows])
            part, gain_row = rms_back(d_query, mixed[rows, columns], gains[0:1, 2 * D :])
            query_gain = query_gain + gain_row
            d_mixed[rows, columns] = part.astype(bf16)
        d_keyvals[i, :, :HD] = d_keys * scale
        d_keyvals[i, :, HD:] = d_values
    gain_grads[0:1, 2 * D :] = query_gain
    outgoing[...] = d_keyvals[:, : reach * stretch].astype(bf16)
    copies = []
    for i in range(seqs):
        for step, device in enumerate(devices):
            copy = pltpu.make_async_remote_copy(
                src_ref=outgoing.at[i, pl.ds((reach - 1 - step) * stretch, stretch)],
                dst_ref=incoming.at[i, step],
                send_sem=send_sem.at[i, step],
                recv_sem=recv_sem.at[i, step],
                device_id=device,
                device_id_type=MESH,
            )
            copy.start()
            copies.append(copy)
    for copy in copies:
        copy.wait_recv()
    key_gain = jnp.zeros((1, HD), f32)
    for i in range(seqs):
        rows = slice(i * stretch, (i + 1) * stretch)
        own = d_keyvals[i, reach * stretch :]
        for step in range(reach):
            own = own + incoming[i, step].astype(f32)
        d_key = turn(own[:, :HD], cosine[rows], -sine[rows])
        part, gain_row = rms_back(
            d_key, mixed[rows, HEADS * HD : HEADS * HD + HD], gains[1:2, 2 * D :]
        )
        key_gain = key_gain + gain_row
        d_mixed[rows, HEADS * HD : HEADS * HD + HD] = part.astype(bf16)
        d_mixed[rows, HEADS * HD + HD :] = own[:, HD:].astype(bf16)
    gain_grads[1:2, 2 * D :] = key_gain
    d_normed = lax.dot_general(d_mixed[...], w_mixed[...], ACROSS, preferred_element_type=f32)
    part, gain_row = rms_back(d_normed, hidden[...], gains[0:1, :D])
    gain_grads[0:1, :D] = gain_row
    grad[...] = grad[...] + part
    if chained:
        part, gain_row = rms_back(grad[...], down[...], before[1:2, D : 2 * D])
        d_down[...] = part.astype(bf16)
        d_post[...] = gain_row
    for copy in copies:
        copy.wait_send()


def attn_backward(
    d_ffn, above, kept, weights, gains, tables, bias, planes, reach, ident, earlier=None
):
    tokens = above.shape[0]
    seqs, stretch, key_len = bias.shape
    shape = jax.ShapeDtypeStruct
    operands = [d_ffn, above, *kept, *weights, gains, *tables, bias] + list(earlier or [])
    outs = [
        shape((tokens, D), f32),
        shape((tokens, weights[0].shape[1]), bf16),
        shape((tokens, D), bf16),
        shape(gains.shape, f32),
    ]
    if earlier is not None:
        outs += [shape((tokens, D), bf16), shape((1, D), f32)]
    here = pl.BlockSpec(memory_space=pltpu.VMEM)
    vmem, dma = pltpu.VMEM, pltpu.SemaphoreType.DMA
    return pl.pallas_call(
        partial(attn_backward_kernel, planes, reach, earlier is not None),
        out_shape=outs,
        in_specs=[here] * len(operands),
        out_specs=[here] * len(outs),
        scratch_shapes=[
            vmem((seqs, key_len, 2 * HD), f32),
            vmem((seqs, reach * stretch, 2 * HD), bf16),
            vmem((seqs, reach, stretch, 2 * HD), bf16),
            vmem((tokens, HEADS * HD), bf16),
            dma((seqs, reach)),
            dma((seqs, reach)),
        ],
        compiler_params=pltpu.CompilerParams(
            collective_id=ident, has_side_effects=True, vmem_limit_bytes=56 * 2**20
        ),
    )(*operands)


GELU_SLOPE = math.sqrt(2.0 / math.pi)
GELU_CUBE = 0.044715
ACROSS = (((1,), (1,)), ((), ()))
ALONG = (((0,), (0,)), ((), ()))


class Plane:
    def __init__(self, own, bufs, sems):
        self.own = own
        self.rows, self.partial, self.other, self.lands, self.sums, self.arrived = bufs
        self.x_send, self.x_recv, self.f_send, self.f_recv = sems[:4]
        self.c_send, self.c_recv, self.p_send, self.p_recv, self.first = sems[4:]
        self.tp = lax.axis_index("tp")
        self.sibling = {"head": 1 - lax.axis_index("head")}

    def member(self, m):
        tp = self.tp
        upper = lax.rem(lax.div(tp, 2) + lax.div(m, 2), 2)
        lower = lax.rem(lax.rem(tp, 2) + lax.rem(m, 2), 2)
        return {"tp": upper * 2 + lower}

    def remote(self, src, dst, send, recv, device):
        return pltpu.make_async_remote_copy(
            src_ref=src,
            dst_ref=dst,
            send_sem=send,
            recv_sem=recv,
            device_id=device,
            device_id_type=MESH,
        )

    def push(self, m):
        return self.remote(
            self.own, self.rows.at[0, m], self.x_send.at[m], self.x_recv.at[m], self.member(m)
        )

    def keep(self):
        return pltpu.make_async_copy(self.own, self.rows.at[0, 0], self.first)

    def forward(self, m):
        return self.remote(
            self.rows.at[0, m],
            self.rows.at[1, m],
            self.f_send.at[m],
            self.f_recv.at[m],
            self.sibling,
        )

    def cross(self, m):
        return self.remote(
            self.other.at[m], self.lands.at[m], self.c_send.at[m], self.c_recv.at[m], self.sibling
        )

    def home(self, m):
        return self.remote(
            self.sums.at[m],
            self.arrived.at[m],
            self.p_send.at[m],
            self.p_recv.at[m],
            self.member(m),
        )

    def begin(self):
        self.keep().start()
        enter([self.sibling] + [self.member(jnp.int32(m)) for m in range(1, PLANE)])
        for m in range(1, PLANE):
            self.push(jnp.int32(m)).start()

    def work(self, compute):
        def settle(m):
            self.cross(m).wait_recv()

            def add(rows):
                value = self.partial[m, rows] + self.lands[m, rows].astype(f32)
                self.sums[m, rows] = value.astype(bf16)

            by_rows(self.partial.shape[1], add)
            self.home(m).start()

        def step(m, carry):
            @pl.when(m == 0)
            def _():
                self.keep().wait()

            @pl.when(m > 0)
            def _():
                self.push(m).wait_recv()

            self.forward(m).start()
            self.partial[m] = compute(0, m)
            self.forward(m).wait_recv()
            self.other[m] = compute(1, m).astype(bf16)
            self.cross(m).start()

            @pl.when(m >= 2)
            def _():
                settle(m - 1)

            return carry

        lax.fori_loop(0, PLANE, step, 0)
        settle(jnp.int32(PLANE - 1))

    def finish(self, result):
        self.cross(jnp.int32(0)).wait_recv()
        for m in range(1, PLANE):
            self.home(jnp.int32(m)).wait_recv()

        def add(rows):
            value = self.partial[0, rows] + self.lands[0, rows].astype(f32)
            for m in range(1, PLANE):
                value = value + self.arrived[m, rows].astype(f32)
            result[rows] = value

        by_rows(result.shape[0], add)
        for m in range(PLANE):
            m = jnp.int32(m)
            self.forward(m).wait_send()
            self.cross(m).wait_send()
        for m in range(1, PLANE):
            m = jnp.int32(m)
            self.push(m).wait_send()
            self.home(m).wait_send()


def chunks(extent, step=256):
    return [slice(at, min(at + step, extent)) for at in range(0, extent, step)]


def gate_up_copies(gu_ref, gate_up, sem):
    blocks = gu_ref.shape[0]
    rows = gate_up.shape[1] // blocks
    return [
        pltpu.make_async_copy(
            gu_ref.at[block, part],
            gate_up.at[part, pl.ds(block * rows, rows)],
            sem.at[2 * block + part],
        )
        for block in range(blocks)
        for part in range(2)
    ]


def ffn_forward_kernel(own, gu_ref, halves_ref, group, saved_down, result, *scratch):
    rows, gate_up, down = scratch[:3]
    plane = Plane(own, (rows,) + scratch[3:8], scratch[8:17])
    weight_sem, group_sem, halves, half_send, half_recv, half_own, save_sem = scratch[17:]
    core = lax.axis_index("head")
    share, width = halves.shape[1:]
    copies = gate_up_copies(gu_ref, gate_up, weight_sem)
    copies.append(
        pltpu.make_async_copy(
            halves_ref.at[0, pl.ds(pl.multiple_of(core * share, 16), share)],
            halves.at[core],
            half_own,
        )
    )
    for copy in copies:
        copy.start()
    plane.begin()
    half = plane.remote(
        halves_ref.at[0, pl.ds(pl.multiple_of((1 - core) * share, 16), share)],
        halves.at[core],
        half_send,
        half_recv,
        plane.sibling,
    )
    half.start()
    for copy in copies:
        copy.wait()
    pltpu.make_async_remote_copy(
        src_ref=halves_ref.at[0, pl.ds(pl.multiple_of((1 - core) * share, 16), share)],
        dst_ref=halves.at[1 - core],
        send_sem=half_send,
        recv_sem=half_recv,
        device_id=plane.sibling,
        device_id_type=MESH,
    ).wait_recv()

    def join(at):
        down[at] = jnp.concatenate([halves[h, at] for h in range(2)], axis=1)

    by_rows(share, join, 32)
    keep_down = pltpu.make_async_copy(down, saved_down, save_sem)
    keep_down.start()

    def compute(side, m):
        tokens, total = rows[side, m], None
        for columns in chunks(share):
            gate = matmul(tokens, gate_up[0, :, columns])
            up = matmul(tokens, gate_up[1, :, columns])
            bend = jnp.tanh(GELU_SLOPE * (gate + GELU_CUBE * (gate * gate * gate)))
            inner = (0.5 * gate * (1.0 + bend) * up).astype(bf16)
            part = matmul(inner, down[columns])
            total = part if total is None else total + part
        return total

    plane.work(compute)
    save = pltpu.make_async_copy(rows, group, group_sem)
    save.start()
    plane.finish(result)
    save.wait()
    keep_down.wait()
    half.wait_send()


def ffn_backward_kernel(
    own, group, gu_ref, down_ref, result, grad_gu, grad_down, *scratch
):
    rows, gate_up, down = scratch[:3]
    plane = Plane(own, (rows,) + scratch[3:8], scratch[8:17])
    weight_sem, group_sem, saved, d_gate, d_up, inner = scratch[17:23]
    down_sem, turned, down_halves, half_send, half_recv, half_own = scratch[23:29]
    share = down.shape[0]
    core = lax.axis_index("head")
    copies = gate_up_copies(gu_ref, gate_up, weight_sem)
    copies.append(pltpu.make_async_copy(down_ref, down, down_sem))
    for copy in copies:
        copy.start()
    load = pltpu.make_async_copy(group, saved, group_sem)
    load.start()
    plane.begin()
    for copy in copies:
        copy.wait()
    load.wait()

    def recompute(index, carry):
        side, m = lax.div(index, PLANE), lax.rem(index, PLANE)
        tokens = saved[side, m]
        for columns in chunks(share):
            gate = matmul(tokens, gate_up[0, :, columns])
            up = matmul(tokens, gate_up[1, :, columns])
            square = gate * gate
            bend = jnp.tanh(GELU_SLOPE * (gate + GELU_CUBE * (square * gate)))
            half = 0.5 * (1.0 + bend)
            value = gate * half
            slope = half + (0.5 * GELU_SLOPE) * gate * (1.0 - bend * bend) * (
                1.0 + (3.0 * GELU_CUBE) * square
            )
            inner[side, m, :, columns] = (value * up).astype(bf16)
            d_gate[side, m, :, columns] = (slope * up).astype(bf16)
            d_up[side, m, :, columns] = value.astype(bf16)
        return carry

    lax.fori_loop(0, 2 * PLANE, recompute, 0)

    def compute(side, m):
        tokens, total = rows[side, m], None
        for columns in chunks(share):
            d_inner = lax.dot_general(tokens, down[columns], ACROSS, preferred_element_type=f32)
            gate = (d_inner * d_gate[side, m, :, columns].astype(f32)).astype(bf16)
            up = (d_inner * d_up[side, m, :, columns].astype(f32)).astype(bf16)
            d_gate[side, m, :, columns] = gate
            d_up[side, m, :, columns] = up
            part = lax.dot_general(
                gate, gate_up[0, :, columns], ACROSS, preferred_element_type=f32
            ) + lax.dot_general(up, gate_up[1, :, columns], ACROSS, preferred_element_type=f32)
            total = part if total is None else total + part
        return total

    plane.work(compute)
    width = rows.shape[-1]
    step = width // 3

    by_planes = len(grad_gu.shape) == 4
    sides = scratch[29] if by_planes else grad_gu

    def tall(ref, columns=slice(None)):
        value = ref[:, :, :, columns]
        return value.reshape(-1, value.shape[-1])

    @pl.loop(0, 3)
    def _(index):
        at = pl.ds(pl.multiple_of(index * step, step), step)
        tokens = tall(saved, at)
        for part, other in enumerate((d_gate, d_up)):
            sides[part, at] = lax.dot_general(
                tokens, tall(other), ALONG, preferred_element_type=f32
            ).astype(bf16)
        turned[at] = lax.dot_general(
            tall(rows, at), tall(inner), ALONG, preferred_element_type=f32
        ).astype(bf16)

    stores = []
    if by_planes:
        for plane_at in range(grad_gu.shape[0]):
            for part in range(2):
                height = grad_gu.shape[2]
                copy = pltpu.make_async_copy(
                    sides.at[part, pl.ds(plane_at * height, height)],
                    grad_gu.at[plane_at, part],
                    scratch[30].at[2 * plane_at + part],
                )
                copy.start()
                stores.append(copy)
    half_width = down_halves.shape[2]
    for h in range(2):
        down_halves[h] = turned[h * half_width : (h + 1) * half_width].T
    half = plane.remote(
        down_halves.at[1 - core], grad_down.at[core], half_send, half_recv, plane.sibling
    )
    half.start()
    stay = pltpu.make_async_copy(down_halves.at[core], grad_down.at[core], half_own)
    stay.start()
    plane.finish(result)
    half.wait()
    stay.wait()
    for copy in stores:
        copy.wait()


def ffn(own, weights, ident, planes, group=None):
    gate_up, down = weights
    tokens, width = own.shape
    blocks, _, _, share = gate_up.shape
    vmem, dma = pltpu.VMEM, pltpu.SemaphoreType.DMA
    scratch = [
        vmem((2, PLANE, tokens, width), bf16),
        vmem((2, width, share), bf16),
        vmem((share, width), bf16),
        vmem((PLANE, tokens, width), f32),
    ]
    scratch += [vmem((PLANE, tokens, width), bf16)] * 4
    scratch += [dma((PLANE,))] * 8 + [dma, dma((2 * blocks,)), dma]
    here, there = pl.BlockSpec(memory_space=pltpu.VMEM), pl.BlockSpec(memory_space=pl.ANY)
    shape = jax.ShapeDtypeStruct
    summed = shape((tokens, width), f32)
    if group is None:
        kernel, operands = ffn_forward_kernel, (own, gate_up, down)
        in_specs, out_specs = [here, there, there], [there, there, here]
        out_shape = [
            shape((2, PLANE, tokens, width), bf16),
            shape((share, width), bf16),
            summed,
        ]
        scratch += [vmem((2, share, width // 2), bf16)] + [dma] * 4
    else:
        kernel, operands = ffn_backward_kernel, (own, group, gate_up, down)
        by_planes = width // planes % 16 == 0
        sides = (2, width, share)
        in_specs = [here, there, there, there]
        out_specs = [here, there if by_planes else here, there]
        out_shape = [
            summed,
            shape((planes, 2, width // planes, share) if by_planes else sides, bf16),
            shape((2, share, width // 2), bf16),
        ]
        scratch += [vmem((2, PLANE, tokens, width), bf16)]
        scratch += [vmem((2, PLANE, tokens, share), bf16)] * 3
        scratch += [dma, vmem((width, share), bf16), vmem((2, share, width // 2), bf16)]
        scratch += [dma] * 3
        if by_planes:
            scratch += [vmem(sides, bf16), dma((2 * planes,))]
    return pl.pallas_call(
        kernel,
        out_shape=out_shape,
        in_specs=in_specs,
        out_specs=out_specs,
        scratch_shapes=scratch,
        cost_estimate=LIGHT,
        compiler_params=pltpu.CompilerParams(
            collective_id=ident, has_side_effects=True, vmem_limit_bytes=60 * 2**20
        ),
    )(*operands)


def exact(left, right, dims=(((1,), (0,)), ((), ()))):
    return lax.dot_general(
        left, right, dims, precision=finest_precision, preferred_element_type=f32
    )


def update_kernel(sizes, counts, *refs):
    cores, planes, members = sizes
    rest = list(refs)
    take = lambda number: [rest.pop(0) for _ in range(number)]
    plain = [take(number) for number in counts]
    sides = take(cores)
    moments_in, weights_in, weights_out, moments_out = (take(4) for _ in range(4))
    moment, weight, gram, land, factor = (take(4) for _ in range(5))
    pieces, arrived = take(2)
    load_sem, store_sem, gram_send, gram_recv, factor_send, factor_recv = take(6)
    gu_send, gu_recv, gu_own = take(3)
    core, _, tp = (lax.axis_index(axis) for axis in EVERY)
    sibling = {"head": 1 - core}
    order = (0, 1, 3, 2)
    loads = {}
    for k in range(4):
        for part, source, target in ((0, moments_in, moment), (1, weights_in, weight)):
            copy = pltpu.make_async_copy(source[k], target[k], load_sem.at[part, k])
            copy.start()
            loads[part, k] = copy
    group = []
    for step in range(1, cores * members):
        far = lax.rem(core + step // members, cores), lax.rem(tp + step % members, members)
        group.append((dict(zip(GROUP, far)), linear(far, (cores, members))))
    enter([device for device, _ in group])
    rows = moment[2].shape[1]
    for part in range(cores):
        for j in range(members):
            for layer in range(cores):
                at = (part * members + j) * rows
                pieces[part * members + j, layer * rows : (layer + 1) * rows] = sides[layer][
                    at : at + rows
                ]
    if pieces.shape[1] > cores * rows:
        for piece in range(cores * members):
            pieces[piece, cores * rows :] = jnp.zeros(
                (pieces.shape[1] - cores * rows, pieces.shape[2]), bf16
            )
    me = linear((core, tp), (cores, members))
    moves, stores = [], []

    def send(src, dst, send_sem, recv_sem, device):
        copy = pltpu.make_async_remote_copy(
            src_ref=src,
            dst_ref=dst,
            send_sem=send_sem,
            recv_sem=recv_sem,
            device_id=device,
            device_id_type=MESH,
        )
        copy.start()
        return copy

    for step, (device, index) in enumerate(group):
        moves.append(
            send(pieces.at[index], arrived.at[me], gu_send.at[step], gu_recv.at[step], device)
        )
    own = pltpu.make_async_copy(pieces.at[me], arrived.at[me], gu_own)
    own.start()

    def store(part, k):
        source, target = (moment, moments_out) if part == 0 else (weight, weights_out)
        copy = pltpu.make_async_copy(source[k], target[k], store_sem.at[part, k])
        copy.start()
        stores.append(copy)

    def gram_of(k):
        def one(layer, carry):
            gram[k][layer] = exact(moment[k][layer], moment[k][layer], ACROSS)
            return carry

        lax.fori_loop(0, cores, one, 0)
        return send(
            gram[k].at[1 - core], land[k], gram_send.at[k], gram_recv.at[k], sibling
        )

    def unit(size):
        down = lax.broadcasted_iota(jnp.int32, (size, size), 0)
        return (down == lax.broadcasted_iota(jnp.int32, (size, size), 1)).astype(f32)

    def orthogonal(members_of):
        for k in members_of:
            total = gram[k][core] + land[k][...]
            one = unit(total.shape[0])
            trace = jnp.sum(jnp.sum(total * one, axis=1, keepdims=True), axis=0, keepdims=True)
            scale = 1.0 / (jnp.sqrt(trace) + 1e-07)
            land[k][...] = total * (scale * scale)
            factor[k][core] = one * scale

        def polynomial(present):
            square = exact(present, present)
            return newton_one * unit(present.shape[0]) + newton_two * present + (
                newton_three * square
            )

        def step(_, carry):
            for k in members_of:
                present = land[k][...]
                poly = polynomial(present)
                factor[k][core] = exact(poly, factor[k][core])
                land[k][...] = exact(exact(poly, present), poly)
            return carry

        lax.fori_loop(0, NS_ITERS - 1, step, 0)
        for k in members_of:
            factor[k][core] = exact(polynomial(land[k][...]), factor[k][core])
        return [
            send(factor[k].at[core], factor[k].at[core], factor_send.at[k], factor_recv.at[k], sibling)
            for k in members_of
        ]

    def apply(k):
        columns = weight[k].shape[2] * cores
        rate = muon_rate * muon_scale * math.sqrt(columns)

        def one(layer, carry):
            weight[k][layer] = weight[k][layer] * (1.0 - muon_rate * muon_shrink) - rate * exact(
                factor[k][layer], moment[k][layer]
            )
            return carry

        lax.fori_loop(0, cores, one, 0)
        store(1, k)

    def arrive(copies):
        for copy in copies:
            copy.wait_recv()

    sent = []
    for index, k in enumerate(order[:3]):
        loads[0, k].wait()
        height = moment[k].shape[1]
        for layer in range(cores):
            if len(plain[index]) == 1:
                gradient = plain[index][0][layer * height : (layer + 1) * height]
            else:
                gradient = plain[index][layer][...].astype(f32)
            moment[k][layer] = muon_decay * moment[k][layer] + gradient
        store(0, k)
        sent.append(gram_of(k))
    arrive(sent)
    crossed = orthogonal(order[:3])
    sent += crossed
    own.wait()
    for copy in moves:
        copy.wait_recv()
    loads[0, 2].wait()
    half = planes // cores
    block = arrived.shape[2] // half
    for layer in range(cores):
        cut = [
            arrived[
                c * members + j,
                layer * rows : (layer + 1) * rows,
                k * block : (k + 1) * block,
            ].astype(f32)
            for c in range(cores)
            for k in range(half)
            for j in range(members)
        ]
        moment[2][layer] = muon_decay * moment[2][layer] + jnp.concatenate(cut, axis=1)
    store(0, 2)
    last = gram_of(2)
    sent.append(last)
    arrive(crossed)
    for k in range(4):
        loads[1, k].wait()
    for k in order[:3]:
        apply(k)
    arrive([last])
    crossed = orthogonal(order[3:])
    sent += crossed
    arrive(crossed)
    apply(2)
    for copy in moves + sent:
        copy.wait_send()
    for copy in stores:
        copy.wait()


def update(gradients, sides, moments, weights, ident):
    sizes = tuple(lax.axis_size(axis) for axis in EVERY)
    cores, planes, members = sizes
    vmem, dma = pltpu.VMEM, pltpu.SemaphoreType.DMA
    layers, rows, columns = moments[2].shape
    piece = (
        cores * members,
        -(-layers * rows // 16) * 16,
        columns // (cores * members),
    )
    shapes = [m.shape for m in moments]
    square = [(s[1], s[1]) for s in shapes]
    scratch = [vmem(s, f32) for s in shapes] * 2
    scratch += [vmem((layers,) + s, f32) for s in square]
    scratch += [vmem(s, f32) for s in square]
    scratch += [vmem((layers,) + s, f32) for s in square]
    scratch += [vmem(piece, bf16)] * 2
    scratch += [dma((2, 4))] * 2 + [dma((4,))] * 4
    scratch += [dma((cores * members - 1,))] * 2 + [dma]
    here, there = pl.BlockSpec(memory_space=pltpu.VMEM), pl.BlockSpec(memory_space=pl.ANY)
    operands = sum(gradients, []) + sides
    return pl.pallas_call(
        partial(update_kernel, sizes, [len(g) for g in gradients]),
        out_shape=[jax.ShapeDtypeStruct(s, f32) for s in shapes] * 2,
        in_specs=[here] * len(operands) + [there] * 8,
        out_specs=[there] * 8,
        scratch_shapes=scratch,
        compiler_params=pltpu.CompilerParams(
            collective_id=ident, has_side_effects=True, vmem_limit_bytes=56 * 2**20
        ),
    )(*operands, *moments, *weights)


def padded(array, multiple=16):
    extra = -array.shape[-2] % multiple
    if extra == 0:
        return array
    return jnp.pad(array, [(0, 0)] * (array.ndim - 2) + [(0, extra), (0, 0)])


def rms_norm(values, norm_gain):
    return (
        values * lax.rsqrt(jnp.mean(values * values, axis=-1, keepdims=True) + norm_eps) * norm_gain
    )


def rope_tables(positions, head_dim):
    half_dim = head_dim // 2
    frequency = jnp.exp(
        jnp.arange(half_dim, dtype=jnp.float32) * (-2.0 * math.log(rope_base) / head_dim)
    )
    angles = positions.astype(jnp.float32)[:, None] * frequency[None, :]
    return (jnp.cos(angles), jnp.sin(angles))


def matmul(left, right):
    return jnp.dot(left, right, preferred_element_type=f32)


def body(
    inputs,
    cotangent,
    teacher,
    segments,
    valid_mask,
    w_qkv,
    w_out,
    w_gu,
    w_down,
    norm_gains,
    mom_qkv,
    mom_out,
    mom_gu,
    mom_down,
    gain_first,
    gain_second,
):
    cores = lax.axis_size("head")
    planes = lax.axis_size("zd")
    seq_devices = planes * PLANE
    core = lax.axis_index("head")
    seq_place = lax.axis_index("zd") * PLANE + lax.axis_index("tp")
    half_seqs, stretch_len = inputs.shape[:2]
    tokens = half_seqs * stretch_len
    all_seqs = half_seqs * cores
    seq_length = stretch_len * seq_devices
    reach = -(-WINDOW // stretch_len)
    key_len = (reach + 1) * stretch_len
    qkv_rows, qkv_cols = w_qkv.shape[1:]
    out_rows, out_cols = w_out.shape[1:]
    gu_rows = w_gu.shape[1]
    ff_block = w_down.shape[1]
    share = FF // (cores * PLANE)
    half_planes = planes // cores
    gain_cols = norm_gains.shape[-1]
    gain_len = gain_cols * seq_devices
    lanes = -(-gain_cols // 128) * 128

    packet = jnp.zeros((8, lanes), f32)
    packet = packet.at[:LAYERS, :gain_cols].set(norm_gains[:, 0].astype(bf16).astype(f32))
    packet = packet.at[LAYERS, 0].set(jnp.sum(valid_mask.astype(f32)))
    gu_pieces, w_mixed, w_project, packets, *later = start(
        w_gu, w_qkv, w_out, packet, 0
    )
    attn_weights = [w_mixed, w_project]
    gu_pieces = gu_pieces[:, : LAYERS * gu_rows].reshape(cores * PLANE, LAYERS, gu_rows, share)
    packets = packets.reshape(cores, seq_devices, 8, lanes)
    valid_count = jnp.sum(packets[:, :, LAYERS, 0])
    gain_rows = [
        packets[:, :, layer, :gain_cols].reshape(cores, gain_len) for layer in range(LAYERS)
    ]

    def gate_up_rows(layer):
        pieces = gu_pieces[:, layer].reshape(2, PLANE * gu_rows, share)
        pieces = lax.all_gather(pieces, "zd", axis=0)
        if PLANE * gu_rows % 16:
            pieces = pieces.transpose(1, 0, 2, 3).reshape(1, 2, D, share)
        return pieces

    def down_rows(layer):
        rows = w_down[layer : layer + 1].astype(bf16)
        return lax.all_gather(rows, "zd", axis=1, tiled=True)

    full = [(gate_up_rows(0), down_rows(0))] + [None] * (LAYERS - 1)

    own_places = seq_place * stretch_len + jnp.arange(stretch_len, dtype=jnp.int32)
    key_places = (seq_place - reach) * stretch_len + jnp.arange(key_len, dtype=jnp.int32)
    cosine_table, sine_table = rope_tables(own_places, HD)
    own_rows = lax.dynamic_slice_in_dim(segments, core * half_seqs, half_seqs, 0)
    own_segments = lax.dynamic_slice_in_dim(own_rows, seq_place * stretch_len, stretch_len, 1)
    padded_segments = jnp.pad(own_rows, ((0, 0), (reach * stretch_len, 0)), constant_values=-1)
    key_segments = lax.dynamic_slice_in_dim(padded_segments, seq_place * stretch_len, key_len, 1)
    spacing = own_places[:, None] - key_places[None, :]
    allowed = (spacing >= 0) & (spacing < WINDOW) & (key_places[None, :] >= 0)
    allowed = allowed[None] & (own_segments[:, :, None] == key_segments[:, None, :])

    tables = [jnp.tile(t, (half_seqs, 1)) for t in (cosine_table, sine_table)]
    bias = jnp.where(allowed, 0.0, -1e30).astype(f32)

    saved, previous = [], None
    base = inputs.reshape(tokens, D)
    for layer in range(LAYERS):
        weights = list(attn_weights)
        hidden, normed, mixed, queries, keyvals, attended, projected, half, normed_ffn = attn_forward(
            base, weights, gain_rows[layer], tables, bias, planes, reach, 3 + layer, previous
        )
        ffn_share = full[layer]
        if layer + 1 < LAYERS:
            gu_pieces, w_down, later, attended = lax.optimization_barrier(
                (gu_pieces, w_down, later, attended)
            )
            attn_weights = later_weights(later, w_qkv, w_out, layer + 1, 2 + 20 * layer)
            full[layer + 1] = (gate_up_rows(layer + 1), down_rows(layer + 1))
            normed_ffn, *attn_weights = lax.optimization_barrier((normed_ffn, *attn_weights))
        group_normed, whole_down, down_out = ffn(normed_ffn, ffn_share, 5 + layer, planes)
        full[layer] = (weights, (ffn_share[0], whole_down))
        saved.append(
            (
                [hidden, mixed, queries, keyvals, projected, half],
                [normed, attended],
                group_normed,
                down_out,
            )
        )
        base, previous = half, (down_out, gain_rows[layer])

    output, post_ffn_back = jax.vjp(rms_norm, down_out, gain_rows[-1][1, D : 2 * D])
    output = base + output
    target_gap = output - teacher.reshape(tokens, D).astype(f32)
    valid_weight = valid_mask.astype(f32).reshape(tokens, 1)
    square_sum = jnp.sum(valid_weight * target_gap * target_gap)
    loss_weight = float(all_seqs * seq_length * D // 4)
    grad_hidden = (
        cotangent.reshape(tokens, D).astype(f32)
        + 2.0 * loss_weight / (valid_count * D) * valid_weight * target_gap
    )
    d_down, d_post_ffn = post_ffn_back(grad_hidden)
    d_down, d_post_ffn = d_down.astype(bf16), d_post_ffn[None]

    tiled = ff_block % 16 == 0
    attn_acts = [None] * LAYERS
    down_grads = [None] * LAYERS
    gain_grads = [None] * LAYERS
    gu_sums = [None] * LAYERS
    for layer in reversed(range(LAYERS)):
        kept, (normed, attended), group_normed, _ = saved[layer]
        weights, ffn_share = full[layer]
        d_normed_ffn, grad_gu, grad_down = ffn(
            d_down, ffn_share, 9 + layer, planes, group_normed
        )
        if layer == 0 and tiled:
            first_down = grad_down.reshape(planes, ff_block, out_cols)
        else:
            down_grads[layer] = lax.psum_scatter(
                grad_down.reshape(planes * ff_block, out_cols),
                "zd",
                scatter_dimension=0,
                tiled=True,
            )
        if len(grad_gu.shape) == 3:
            grad_gu = grad_gu.reshape(2, planes, PLANE * gu_rows, share).transpose(1, 0, 2, 3)
        gu_sums[layer] = lax.psum_scatter(
            grad_gu.reshape(-1, share), "zd", scatter_dimension=0, tiled=True
        )
        earlier = (saved[layer - 1][3], gain_rows[layer - 1]) if layer > 0 else None
        grad_hidden, d_mixed, d_projected, gain_grads[layer], *d_rest = attn_backward(
            d_normed_ffn,
            grad_hidden,
            kept,
            weights,
            gain_rows[layer],
            tables,
            bias,
            planes,
            reach,
            17 + layer,
            earlier,
        )
        gain_grads[layer] = gain_grads[layer].at[1:, D : 2 * D].set(d_post_ffn)
        if layer > 0:
            d_down, d_post_ffn = d_rest
        attn_acts[layer] = [normed, d_mixed, attended, d_projected]
    attn_acts[0][1], gu_sums[1:], down_grads[1:] = lax.optimization_barrier(
        (attn_acts[0][1], gu_sums[1:], down_grads[1:])
    )

    packet = jnp.stack(gain_grads, axis=1).reshape(cores, LAYERS, planes, PLANE, gain_cols)
    packet = packet.transpose(0, 3, 2, 1, 4)
    packet = jnp.pad(packet, [(0, 0)] * 3 + [(0, 8 - LAYERS), (0, lanes - gain_cols)])
    packet = packet.at[:, :, :, LAYERS, 0].set(square_sum)
    packet = packet.reshape(cores, PLANE, planes * 8, lanes)
    down = first_down if tiled else None
    grad_qkv, grad_out, packet, *summed_down = collect(sum(attn_acts, []), packet, down, 19)
    if tiled:
        (down_grads[0],) = summed_down
    mse_loss = packet[LAYERS, 0] / (valid_count * D)
    gain_grad = packet[:LAYERS, None, :gain_cols]

    outcome = update(
        [[grad_qkv], [grad_out], down_grads],
        gu_sums,
        (mom_qkv, mom_out, mom_gu, mom_down),
        (w_qkv, w_out, w_gu, w_down),
        15,
    )
    new_weights, moments = outcome[:4], outcome[4:]
    gain_first_new = beta_one * gain_first + (1.0 - beta_one) * gain_grad
    gain_second_new = beta_two * gain_second + (1.0 - beta_two) * gain_grad * gain_grad
    gains_new = norm_gains - adam_rate * (gain_first_new / (1.0 - beta_one**STEP)) / (
        jnp.sqrt(gain_second_new / (1.0 - beta_two**STEP)) + adam_epsilon
    )
    return (
        mse_loss,
        output.reshape(inputs.shape),
        grad_hidden.reshape(inputs.shape),
        *new_weights,
        *moments,
        gains_new,
        gain_first_new,
        gain_second_new,
    )


def solution(mesh):
    cores, length = mesh.devices.shape
    split = Mesh(mesh.devices.reshape(cores, length // PLANE, PLANE), EVERY)
    stream = P("head", SEQ, None)
    matrix = P(None, SEQ, "head")
    gains = P(None, "head", SEQ)
    return jax.shard_map(
        body,
        mesh=split,
        in_specs=(stream, stream, stream, P(), P("head", SEQ))
        + (matrix,) * 4
        + (gains,)
        + (matrix,) * 4
        + (gains,) * 2,
        out_specs=(P(), stream, stream) + (matrix,) * 8 + (gains,) * 3,
        check_vma=False,
    )
```

profile of v0, /device:TPU:0, one launch (start us, length us, event | category | flops | bytes accessed | tf_op | source)
XLA Modules:
  0.0 869.8 jit_solution(15954827163162908286)
XLA Ops:
  7.2 2.1 slice.176
  11.4 82.7 %shard_map.263 = (bf16[8,144,864]{2,1,0:T(8,128)(2,1)}, bf16[1152,1536]{1,0:T(8,128)(2,1)}, bf16[1024,1152]{1,0:T(8,128)(2,1)}, f32[2,4,4,8,256]{4,3,2,1,0:T(8,1...) custom-call(f32[2,72,6912]{2,1,0:T(8,128)} %refs_12_.1, f32[2,72,768]{2,1,0:T(8,128)} %refs_10_.1, ...), custom_call_target="tpu_custom_call" | custom-call | tf_op jit(solution)/shard_map/pallas_call | solution.py:269
  94.1 2.3 slice.162
  101.0 29.0 %shard_map.264 = (f32[256,1152]{1,0:T(8,128)}, bf16[256,1152]{1,0:T(8,128)(2,1)}, f32[256,1536]{1,0:T(8,128)}, bf16[256,1024]{1,0:T(8,128)(2,1)}, bf16[1,768,512...) custom-call(bf16[256,1152]{1,0:T(8,128)(2,1)} %bitcast.55, ...), custom_call_target="tpu_custom_call" | custom-call | tf_op jit(solution)/shard_map/pallas_call | solution.py:632
  130.0 2.1 slice.175
  133.5 51.1 %shard_map.265 = (bf16[1152,1536]{1,0:T(8,128)(2,1)}, bf16[1024,1152]{1,0:T(8,128)(2,1)S(1)}) custom-call(bf16[1,4,80,768]{3,2,1,0:T(8,128)(2,1)S(1)} %copy-done.1, bf16[1,4,64,576]{3,2,1,0:T(8,128)(2,1)S(1)} %copy-done.2), custom_call_target="tpu_custom_call" | custom-call | tf_op jit(solution)/shard_map/pallas_call | solution.py:286
  184.6 1.4 copy-done
  186.1 1.5 slice_reduce_fusion.2
  188.4 64.5 %shard_map.266 = (bf16[2,4,256,1152]{3,2,1,0:T(8,128)(2,1)}, bf16[864,1152]{1,0:T(8,128)(2,1)}, f32[256,1152]{1,0:T(8,128)}) custom-call(bf16[256,1152]{1,0:T(8,128)(2,1)} %get-tuple-element.159.own, bf16[4,2,288,864]{3,2,1,0:T(8,128)(2,1)} %all-gather.5.cloned.1.call-done.gu_ref, bf16[1,1728,576]{2,1,0:T(8,128)(2,1)} %all-gather.7.cloned.1.call-done.halves_ref), custom_call_target="tpu_custom_call" | custom-call | flops 1 | bytes 1 | tf_op jit(solution)/shard_map/pallas_call | solution.py:1142
  253.0 41.5 %shard_map.267 = (f32[256,1152]{1,0:T(8,128)}, bf16[256,1152]{1,0:T(8,128)(2,1)}, f32[256,1536]{1,0:T(8,128)}, bf16[256,1024]{1,0:T(8,128)(2,1)}, bf16[1,768,512...) custom-call(f32[256,1152]{1,0:T(8,128)} %get-tuple-element.149.refs_, ...), custom_call_target="tpu_custom_call" | custom-call | tf_op jit(solution)/shard_map/pallas_call | solution.py:632
  294.5 22.1 %all-gather.9.cloned.1.call-done.gu_ref = bf16[4,2,288,864]{3,2,1,0:T(8,128)(2,1)} async-done(((bf16[1,2,288,864]{3,2,1,0:T(8,128)(2,1)}), bf16[4,2,288,864]{3,2,1,0:T(8,128)(2,1)}) %all-gather.9.cloned.1.call-update) | async-done | bytes 3981328 | tf_op jit(solution)/shard_map/all_gather | solution.py:1455
  316.6 75.5 %shard_map.268 = (bf16[2,4,256,1152]{3,2,1,0:T(8,128)(2,1)}, bf16[864,1152]{1,0:T(8,128)(2,1)}, f32[256,1152]{1,0:T(8,128)}) custom-call(bf16[256,1152]{1,0:T(8,128)(2,1)} %get-tuple-element.164.own, bf16[4,2,288,864]{3,2,1,0:T(8,128)(2,1)} %all-gather.9.cloned.1.call-done.gu_ref, bf16[1,1728,576]{2,1,0:T(8,128)(2,1)} %all-gather.11.cloned.1.call-done.halves_ref), custom_call_target="tpu_custom_call" | custom-call | flops 1 | bytes 1 | tf_op jit(solution)/shard_map/pallas_call | solution.py:1142
  392.2 1.5 multiply_reduce_fusion.2
  397.2 77.5 %shard_map.269 = (f32[256,1152]{1,0:T(8,128)}, bf16[4,2,288,864]{3,2,1,0:T(8,128)(2,1)}, bf16[2,864,576]{2,1,0:T(8,128)(2,1)}) custom-call(bf16[256,1152]{1,0:T(8,128)(2,1)} %fusion.own, bf16[2,4,256,1152]{3,2,1,0:T(8,128)(2,1)} %get-tuple-element.168.group, bf16[4,2,288,864]{3,2,1,0:T(8,128)(2,1)} %all-gather.9.cloned.1.call-done.gu_ref, ...), custom_call_target="tpu_custom_call" | custom-call | flops 1 | bytes 1 | tf_op jit(solution)/shard_map/pallas_call | solution.py:1142
  475.6 37.8 %shard_map.270 = (f32[256,1152]{1,0:T(8,128)}, bf16[256,1536]{1,0:T(8,128)(2,1)}, bf16[256,1152]{1,0:T(8,128)(2,1)}, f32[2,2560]{1,0:T(2,128)}, bf16[256,1152]{1,0:T(8,128)(2,1)}, /*index=5*/f32[1,1152]{1,0:T(1,128)}) custom-call(f32[256,1152]{1,0:T(8,128)} %get-tuple-element.170.refs_0_, f32[256,1152]{1,0:T(8,128)} %copy-done.4, ...), custom_call_target="tpu_custom_call" | custom-call | tf_op jit(solution)/shard_map/pallas_call | solution.py:770
  513.4 93.8 %shard_map.271 = (f32[256,1152]{1,0:T(8,128)}, bf16[4,2,288,864]{3,2,1,0:T(8,128)(2,1)}, bf16[2,864,576]{2,1,0:T(8,128)(2,1)}) custom-call(bf16[256,1152]{1,0:T(8,128)(2,1)} %get-tuple-element.176.own, bf16[2,4,256,1152]{3,2,1,0:T(8,128)(2,1)} %get-tuple-element.177.group, bf16[4,2,288,864]{3,2,1,0:T(8,128)(2,1)} %all-gather.5.cloned.1.call-done.gu_ref, ...), custom_call_target="tpu_custom_call" | custom-call | flops 1 | bytes 1 | tf_op jit(solution)/shard_map/pallas_call | solution.py:1142
  607.3 35.6 %shard_map.272 = (f32[256,1152]{1,0:T(8,128)}, bf16[256,1536]{1,0:T(8,128)(2,1)}, bf16[256,1152]{1,0:T(8,128)(2,1)}, f32[2,2560]{1,0:T(2,128)}) custom-call(f32[256,1152]{1,0:T(8,128)} %get-tuple-element.179.refs_0_, f32[256,1152]{1,0:T(8,128)} %get-tuple-element.180.refs_1_, f32[256,1152]{1,0:T(8,128)} %get-tuple-element.181.refs_2_, ...), custom_call_target="tpu_custom_call" | custom-call | tf_op jit(solution)/shard_map/pallas_call | solution.py:770
  642.9 1.4 scatter.30
  647.2 130.3 %shard_map.273 = (f32[144,768]{1,0:T(8,128)}, f32[128,576]{1,0:T(8,128)}, f32[8,256]{1,0:T(8,128)}, f32[432,576]{1,0:T(8,128)}) custom-call(bf16[256,1152]{1,0:T(8,128)(2,1)} %get-tuple-element.148.refs_0_, bf16[256,1536]{1,0:T(8,128)(2,1)} %get-tuple-element.189.refs_1_, bf16[256,1024]{1,0:T(8,128)(2,1)} %get-tuple-element.190.refs_2_, ...), custom_call_target="tpu_custom_call" | custom-call | flops 1 | bytes 1 | tf_op jit(solution)/shard_map/pallas_call | solution.py:506
  777.5 64.4 %shard_map.274 = (f32[2,72,768]{2,1,0:T(8,128)}, f32[2,64,576]{2,1,0:T(8,128)}, f32[2,72,6912]{2,1,0:T(8,128)}, f32[2,432,576]{2,1,0:T(8,128)}, f32[2,72,768]{2,...) custom-call(f32[144,768]{1,0:T(8,128)} %get-tuple-element.202.refs_0_, ...), custom_call_target="tpu_custom_call" | custom-call | tf_op jit(solution)/shard_map/pallas_call | solution.py:1362
  849.0 4.5 copy.85
  853.5 1.4 copy.86
  857.0 2.0 copy.89
  860.0 1.4 copy.90
  (121 shorter events, 24.8 us)
Async XLA Ops:
  7.2 2.3 copy-start.24
  7.2 2.3 copy-start.28
  7.2 181.2 %all-gather.7.cloned.1.call-start = ((), (), s32[]{:S(2)}) async-start(), calls=%async_computation.4 | async-start | bytes 2764800 | tf_op jit(solution)/shard_map/all_gather | solution.py:1462
  9.4 179.0 %all-gather.5.cloned.1.call-start = ((), (), s32[]{:S(2)}) async-start(), calls=%async_computation.3 | async-start | bytes 5160960 | tf_op jit(solution)/shard_map/all_gather | solution.py:1455
  94.1 4.3 copy-start.23
  96.4 198.2 %all-gather.11.cloned.1.call-start = ((), (), s32[]{:S(2)}) async-start(), calls=%async_computation.6 | async-start | bytes 2764800 | tf_op jit(solution)/shard_map/all_gather | solution.py:1462
  101.0 31.3 %copy-start.12 = (bf16[8,144,864]{2,1,0:T(8,128)(2,1)S(1)}, bf16[8,144,864]{2,1,0:T(8,128)(2,1)}, u32[]{:S(2)}) copy-start(bf16[8,144,864]{2,1,0:T(8,128)(2,1)} %get-tuple-element.151) | copy-start | bytes 5971972
  132.2 184.4 %all-gather.9.cloned.1.call-start = ((), (), s32[]{:S(2)}) async-start(), calls=%async_computation.5 | async-start | bytes 5160960 | tf_op jit(solution)/shard_map/all_gather | solution.py:1455
  133.3 513.2 %reduce-scatter.6.cloned.1.call-start = ((), (), s32[]{:S(2)}) async-start(), calls=%async_computation.8 | async-start | bytes 2764800 | tf_op jit(solution)/shard_map/reduce_scatter | solution.py:1534
  186.1 66.9 %copy-start.20 = (f32[2,2560]{1,0:T(2,128)}, f32[2,2560]{1,0:T(2,128)S(1)}, u32[]{:S(2)}) copy-start(f32[2,2560]{1,0:T(2,128)S(1)} %reshape_squeeze.7.refs_5_.refs_10_) | copy-start | bytes 61444
  316.6 77.1 %copy-start.6 = (f32[256,1152]{1,0:T(8,128)S(1)}, f32[256,1152]{1,0:T(8,128)}, u32[]{:S(2)}) copy-start(f32[256,1152]{1,0:T(8,128)} %get-tuple-element.163.refs_7_) | copy-start | bytes 3538948
  316.6 77.1 %copy-start.8 = (bf16[1,256,1152]{2,1,0:T(8,128)(2,1)S(1)}, bf16[1,256,1152]{2,1,0:T(8,128)(2,1)}, u32[]{:S(2)}) copy-start(bf16[1,256,1152]{2,1,0:T(8,128)(2,1)} %param.28) | copy-start | bytes 1769476
  474.8 171.7 %reduce-scatter.4.cloned.1.call-start = ((), (), s32[]{:S(2)}) async-start(), calls=%async_computation.7 | async-start | bytes 5160960 | tf_op jit(solution)/shard_map/reduce_scatter | solution.py:1542
  475.4 302.1 %reduce-scatter.8.cloned.1.call-start = ((), (), s32[]{:S(2)}) async-start(), calls=%async_computation.9 | async-start | bytes 5160960 | tf_op jit(solution)/shard_map/reduce_scatter | solution.py:1542
  607.2 35.7 %copy-start.25 = (f32[1,1152]{1,0:T(1,128)S(1)}, f32[1,1152]{1,0:T(1,128)}, u32[]{:S(2)}) copy-start(f32[1,1152]{1,0:T(1,128)} %get-tuple-element.197) | copy-start | bytes 13828
  607.3 37.1 %copy-start.22 = (f32[2,2560]{1,0:T(2,128)S(1)}, f32[2,2560]{1,0:T(2,128)}, u32[]{:S(2)}) copy-start(f32[2,2560]{1,0:T(2,128)} %get-tuple-element.198) | copy-start | bytes 61444
  777.5 65.7 %copy-start.26 = (f32[2,1,160]{2,1,0:T(1,128)S(1)}, f32[2,1,160]{2,1,0:T(1,128)}, u32[]{:S(2)}) copy-start(f32[2,1,160]{2,1,0:T(1,128)} %param.40) | copy-start | bytes 3844
  777.5 65.7 %copy-start.27 = (f32[2,1,160]{2,1,0:T(1,128)S(1)}, f32[2,1,160]{2,1,0:T(1,128)}, u32[]{:S(2)}) copy-start(f32[2,1,160]{2,1,0:T(1,128)} %param.41) | copy-start | bytes 3844
  777.5 68.8 %copy-start.13 = (f32[256,1152]{1,0:T(8,128)S(1)}, f32[256,1152]{1,0:T(8,128)}, u32[]{:S(2)}) copy-start(f32[256,1152]{1,0:T(8,128)} %get-tuple-element.201) | copy-start | bytes 3538948
  846.3 2.0 copy-start.19
  849.0 4.5 copy-start.11
  853.5 2.1 copy-start.18
  853.5 3.4 copy-start.7
  857.0 3.1 copy-start.10
  (12 other events, 14.2 us)
Sparse Core Ops, SparseCore 0:
  10.2 82.7 all-gather.6
  96.5 79.8 all-gather.4
  178.5 57.5 all-gather.10
  238.1 78.4 all-gather.8
  474.9 54.5 reduce-scatter.5
  531.7 73.3 reduce-scatter.3
  607.5 130.7 reduce-scatter.7
where the time goes:
time: 878 us; the launch traced here: 870 us
  Pallas kernels  784 us (89%)
  local copies, waits for them, and re-layouts  34.4 us (4%)
  waiting for transfers between devices  22.8 us (3%)
  between operations  17.6 us (2%)
  other arithmetic  10.7 us (1%)
    pallas_call x4, Pallas kernels, ffn(): pl.pallas_call(kernel, out_shape=out_shape, in_specs=in_specs, out_specs=...  311 us
    pallas_call x1, Pallas kernels, collect(): pl.pallas_call(partial(collect_kernel, sizes, layers, down is not None),...  130 us
    pallas_call x1, Pallas kernels, start(): pl.pallas_call(partial(start_kernel, sizes), out_shape=outs, in_specs=[he...  82.7 us
    pallas_call x2, Pallas kernels, attn_backward(): pl.pallas_call(partial(attn_backward_kernel, planes, reach, earlier is no...  73.4 us
    pallas_call x2, Pallas kernels, attn_forward(): pl.pallas_call(partial(attn_forward_kernel, planes, reach, earlier is not...  70.6 us
    pallas_call x1, Pallas kernels, update(): pl.pallas_call(partial(update_kernel, sizes, [len(g) for g in gradients])...  64.4 us
    pallas_call x1, Pallas kernels, later_weights(): pl.pallas_call(partial(later_kernel, sizes, layer), out_shape=outs, in_sp...  51.1 us
    all_gather x2, waiting for transfers between devices, gate_up_rows(): pieces = lax.all_gather(pieces, 'zd', axis=0)  22.1 us
  transfers between devices with their start and end apart: 7, of which 1 were waited for; matrix products, arithmetic and copies ran while one was open for 2% of the time, Pallas kernels for 65%

commit v1 on v0

--- a/solution.py
+++ b/solution.py
@@ -525,7 +525,11 @@
         return {"zd": lax.div(there, PLANE), "tp": lax.rem(there, PLANE)}
 
     steps = range(1, reach + 1)
-    return [at(sign * step) for step in steps], [at(-sign * step) for step in steps]
+    devices, sources = [at(sign * step) for step in steps], [at(-sign * step) for step in steps]
+    above = [place + step < total for step in steps]
+    below = [place >= step for step in steps]
+    sends, comes = (above, below) if sign > 0 else (below, above)
+    return devices, sources, sends, comes
 
 
 def inverse_rms(values):
@@ -568,7 +572,7 @@
     attended, projected, hidden_half, normed_ffn = take(4)
     keyvals, send_sem, recv_sem, save_sem = take(4)
     seqs, stretch, key_len = bias.shape
-    devices, sources = neighbours(planes, reach, 1)
+    devices, sources, sends, comes = neighbours(planes, reach, 1)
     enter(devices + sources)
     value = base[...].astype(f32)
     if chained:
@@ -595,15 +599,21 @@
                 device_id=device,
                 device_id_type=MESH,
             )
-            copy.start()
-            copies.append(copy)
+            pl.when(sends[step])(copy.start)
+            copies.append((step, copy))
+
+            @pl.when(jnp.logical_not(comes[step]))
+            def _():
+                at = (reach - 1 - step) * stretch
+                keyvals[i, at : at + stretch] = jnp.zeros((stretch, 2 * HD), bf16)
+
     for h in range(HEADS):
         columns = slice(h * HD, (h + 1) * HD)
         query = mixed[:, columns]
         query = turn(query * inverse_rms(query) * gains[0:1, 2 * D :], cosine[...], sine[...])
         queries[:, columns] = query.astype(bf16)
-    for copy in copies:
-        copy.wait_recv()
+    for step, copy in copies:
+        pl.when(comes[step])(copy.wait_recv)
     save = pltpu.make_async_copy(keyvals, keyvals_out, save_sem)
     save.start()
     for i in range(seqs):
@@ -617,8 +627,8 @@
     half = hidden[...] + out * inverse_rms(out) * gains[0:1, D : 2 * D]
     hidden_half[...] = half
     normed_ffn[...] = (half * inverse_rms(half) * gains[1:2, :D]).astype(bf16)
-    for copy in copies:
-        copy.wait_send()
+    for step, copy in copies:
+        pl.when(sends[step])(copy.wait_send)
     save.wait()
 
 
@@ -668,7 +678,7 @@
         d_down, d_post = take(2)
     d_keyvals, outgoing, incoming, d_attended, send_sem, recv_sem = take(6)
     seqs, stretch, key_len = bias.shape
-    devices, sources = neighbours(planes, reach, -1)
+    devices, sources, sends, comes = neighbours(planes, reach, -1)
     enter(devices + sources)
     scale = 1.0 / math.sqrt(HD)
     part, gain_row = rms_back(d_ffn[...], hidden_half[...], gains[1:2, :D])
@@ -720,10 +730,15 @@
                 device_id=device,
                 device_id_type=MESH,
             )
-            copy.start()
-            copies.append(copy)
-    for copy in copies:
-        copy.wait_recv()
+            pl.when(sends[step])(copy.start)
+            copies.append((step, copy))
+
+            @pl.when(jnp.logical_not(comes[step]))
+            def _():
+                incoming[i, step] = jnp.zeros((stretch, 2 * HD), bf16)
+
+    for step, copy in copies:
+        pl.when(comes[step])(copy.wait_recv)
     key_gain = jnp.zeros((1, HD), f32)
     for i in range(seqs):
         rows = slice(i * stretch, (i + 1) * stretch)
@@ -746,8 +761,8 @@
         part, gain_row = rms_back(grad[...], down[...], before[1:2, D : 2 * D])
         d_down[...] = part.astype(bf16)
         d_post[...] = gain_row
-    for copy in copies:
-        copy.wait_send()
+    for step, copy in copies:
+        pl.when(sends[step])(copy.wait_send)
 
 
 def attn_backward(
@@ -999,7 +1014,6 @@
     plane = Plane(own, (rows,) + scratch[3:8], scratch[8:17])
     weight_sem, group_sem, saved, d_gate, d_up, inner = scratch[17:23]
     down_sem, turned, down_halves, half_send, half_recv, half_own = scratch[23:29]
-    share = down.shape[0]
     core = lax.axis_index("head")
     copies = gate_up_copies(gu_ref, gate_up, weight_sem)
     copies.append(pltpu.make_async_copy(down_ref, down, down_sem))
@@ -1015,36 +1029,31 @@
     def recompute(index, carry):
         side, m = lax.div(index, PLANE), lax.rem(index, PLANE)
         tokens = saved[side, m]
-        for columns in chunks(share):
-            gate = matmul(tokens, gate_up[0, :, columns])
-            up = matmul(tokens, gate_up[1, :, columns])
-            square = gate * gate
-            bend = jnp.tanh(GELU_SLOPE * (gate + GELU_CUBE * (square * gate)))
-            half = 0.5 * (1.0 + bend)
-            value = gate * half
-            slope = half + (0.5 * GELU_SLOPE) * gate * (1.0 - bend * bend) * (
-                1.0 + (3.0 * GELU_CUBE) * square
-            )
-            inner[side, m, :, columns] = (value * up).astype(bf16)
-            d_gate[side, m, :, columns] = (slope * up).astype(bf16)
-            d_up[side, m, :, columns] = value.astype(bf16)
+        gate = matmul(tokens, gate_up[0])
+        up = matmul(tokens, gate_up[1])
+        square = gate * gate
+        bend = jnp.tanh(GELU_SLOPE * (gate + GELU_CUBE * (square * gate)))
+        half = 0.5 * (1.0 + bend)
+        value = gate * half
+        slope = half + (0.5 * GELU_SLOPE) * gate * (1.0 - bend * bend) * (
+            1.0 + (3.0 * GELU_CUBE) * square
+        )
+        inner[side, m] = (value * up).astype(bf16)
+        d_gate[side, m] = (slope * up).astype(bf16)
+        d_up[side, m] = value.astype(bf16)
         return carry
 
     lax.fori_loop(0, 2 * PLANE, recompute, 0)
 
     def compute(side, m):
-        tokens, total = rows[side, m], None
-        for columns in chunks(share):
-            d_inner = lax.dot_general(tokens, down[columns], ACROSS, preferred_element_type=f32)
-            gate = (d_inner * d_gate[side, m, :, columns].astype(f32)).astype(bf16)
-            up = (d_inner * d_up[side, m, :, columns].astype(f32)).astype(bf16)
-            d_gate[side, m, :, columns] = gate
-            d_up[side, m, :, columns] = up
-            part = lax.dot_general(
-                gate, gate_up[0, :, columns], ACROSS, preferred_element_type=f32
-            ) + lax.dot_general(up, gate_up[1, :, columns], ACROSS, preferred_element_type=f32)
-            total = part if total is None else total + part
-        return total
+        d_inner = lax.dot_general(rows[side, m], down[...], ACROSS, preferred_element_type=f32)
+        gate = (d_inner * d_gate[side, m].astype(f32)).astype(bf16)
+        up = (d_inner * d_up[side, m].astype(f32)).astype(bf16)
+        d_gate[side, m] = gate
+        d_up[side, m] = up
+        return lax.dot_general(
+            gate, gate_up[0], ACROSS, preferred_element_type=f32
+        ) + lax.dot_general(up, gate_up[1], ACROSS, preferred_element_type=f32)
 
     plane.work(compute)
     width = rows.shape[-1]

time: 878 us -> 860 us (0.979)
  Pallas kernels: 784 us -> 759 us
    pallas_call x2, Pallas kernels: 73.4 us -> 51.8 us  [attn_backward(): pl.pallas_call(partial(attn_backward_kernel, planes, reach, earlier is no...]
    pallas_call x1, Pallas kernels: 130 us -> 148 us  [collect(): pl.pallas_call(partial(collect_kernel, sizes, layers, down is not None),...]
    pallas_call x2, Pallas kernels: 70.6 us -> 55.3 us  [attn_forward(): pl.pallas_call(partial(attn_forward_kernel, planes, reach, earlier is not...]
    pallas_call x4, Pallas kernels: 311 us -> 300 us  [ffn(): pl.pallas_call(kernel, out_shape=out_shape, in_specs=in_specs, out_specs=...]
where the time goes in v1:
time: 860 us; the launch traced here: 853 us
  Pallas kernels  759 us (88%)
  local copies, waits for them, and re-layouts  34.3 us (4%)
  waiting for transfers between devices  30.2 us (4%)
  between operations  17.6 us (2%)
  other arithmetic  10.7 us (1%)
    pallas_call x4, Pallas kernels, ffn(): pl.pallas_call(kernel, out_shape=out_shape, in_specs=in_specs, out_specs=...  300 us
    pallas_call x1, Pallas kernels, collect(): pl.pallas_call(partial(collect_kernel, sizes, layers, down is not None),...  148 us
    pallas_call x1, Pallas kernels, start(): pl.pallas_call(partial(start_kernel, sizes), out_shape=outs, in_specs=[he...  82.7 us
    pallas_call x1, Pallas kernels, update(): pl.pallas_call(partial(update_kernel, sizes, [len(g) for g in gradients])...  64.4 us
    pallas_call x1, Pallas kernels, later_weights(): pl.pallas_call(partial(later_kernel, sizes, layer), out_shape=outs, in_sp...  56.6 us
    pallas_call x2, Pallas kernels, attn_forward(): pl.pallas_call(partial(attn_forward_kernel, planes, reach, earlier is not...  55.3 us
    pallas_call x2, Pallas kernels, attn_backward(): pl.pallas_call(partial(attn_backward_kernel, planes, reach, earlier is no...  51.8 us
    all_gather x2, waiting for transfers between devices, gate_up_rows(): pieces = lax.all_gather(pieces, 'zd', axis=0)  29.5 us
  transfers between devices with their start and end apart: 7, of which 1 were waited for; matrix products, arithmetic and copies ran while one was open for 2% of the time, Pallas kernels for 65%

profile of v1, /device:TPU:0, one launch (start us, length us, event | category | flops | bytes accessed | tf_op | source)
XLA Modules:
  0.0 852.6 jit_solution(7270265663683846284)
XLA Ops:
  7.2 2.1 slice.176
  11.4 82.7 %shard_map.263 = (bf16[8,144,864]{2,1,0:T(8,128)(2,1)}, bf16[1152,1536]{1,0:T(8,128)(2,1)}, bf16[1024,1152]{1,0:T(8,128)(2,1)}, f32[2,4,4,8,256]{4,3,2,1,0:T(8,1...) custom-call(f32[2,72,6912]{2,1,0:T(8,128)} %refs_12_.1, f32[2,72,768]{2,1,0:T(8,128)} %refs_10_.1, ...), custom_call_target="tpu_custom_call" | custom-call | tf_op jit(solution)/shard_map/pallas_call | solution.py:269
  94.1 2.3 slice.162
  101.0 19.3 %shard_map.264 = (f32[256,1152]{1,0:T(8,128)}, bf16[256,1152]{1,0:T(8,128)(2,1)}, f32[256,1536]{1,0:T(8,128)}, bf16[256,1024]{1,0:T(8,128)(2,1)}, bf16[1,768,512...) custom-call(bf16[256,1152]{1,0:T(8,128)(2,1)} %bitcast.55, ...), custom_call_target="tpu_custom_call" | custom-call | tf_op jit(solution)/shard_map/pallas_call | solution.py:642
  120.3 2.1 slice.175
  124.1 56.6 %shard_map.265 = (bf16[1152,1536]{1,0:T(8,128)(2,1)}, bf16[1024,1152]{1,0:T(8,128)(2,1)S(1)}) custom-call(bf16[1,4,80,768]{3,2,1,0:T(8,128)(2,1)S(1)} %copy-done.1, bf16[1,4,64,576]{3,2,1,0:T(8,128)(2,1)S(1)} %copy-done.2), custom_call_target="tpu_custom_call" | custom-call | tf_op jit(solution)/shard_map/pallas_call | solution.py:286
  180.7 1.4 copy-done
  182.2 1.5 slice_reduce_fusion.2
  184.5 66.6 %shard_map.266 = (bf16[2,4,256,1152]{3,2,1,0:T(8,128)(2,1)}, bf16[864,1152]{1,0:T(8,128)(2,1)}, f32[256,1152]{1,0:T(8,128)}) custom-call(bf16[256,1152]{1,0:T(8,128)(2,1)} %get-tuple-element.159.own, bf16[4,2,288,864]{3,2,1,0:T(8,128)(2,1)} %all-gather.5.cloned.1.call-done.gu_ref, bf16[1,1728,576]{2,1,0:T(8,128)(2,1)} %all-gather.7.cloned.1.call-done.halves_ref), custom_call_target="tpu_custom_call" | custom-call | flops 1 | bytes 1 | tf_op jit(solution)/shard_map/pallas_call | solution.py:1151
  251.1 36.0 %shard_map.267 = (f32[256,1152]{1,0:T(8,128)}, bf16[256,1152]{1,0:T(8,128)(2,1)}, f32[256,1536]{1,0:T(8,128)}, bf16[256,1024]{1,0:T(8,128)(2,1)}, bf16[1,768,512...) custom-call(f32[256,1152]{1,0:T(8,128)} %get-tuple-element.149.refs_, ...), custom_call_target="tpu_custom_call" | custom-call | tf_op jit(solution)/shard_map/pallas_call | solution.py:642
  287.2 29.5 %all-gather.9.cloned.1.call-done.gu_ref = bf16[4,2,288,864]{3,2,1,0:T(8,128)(2,1)} async-done(((bf16[1,2,288,864]{3,2,1,0:T(8,128)(2,1)}), bf16[4,2,288,864]{3,2,1,0:T(8,128)(2,1)}) %all-gather.9.cloned.1.call-update) | async-done | bytes 3981328 | tf_op jit(solution)/shard_map/all_gather | solution.py:1464
  316.7 71.9 %shard_map.268 = (bf16[2,4,256,1152]{3,2,1,0:T(8,128)(2,1)}, bf16[864,1152]{1,0:T(8,128)(2,1)}, f32[256,1152]{1,0:T(8,128)}) custom-call(bf16[256,1152]{1,0:T(8,128)(2,1)} %get-tuple-element.164.own, bf16[4,2,288,864]{3,2,1,0:T(8,128)(2,1)} %all-gather.9.cloned.1.call-done.gu_ref, bf16[1,1728,576]{2,1,0:T(8,128)(2,1)} %all-gather.11.cloned.1.call-done.halves_ref), custom_call_target="tpu_custom_call" | custom-call | flops 1 | bytes 1 | tf_op jit(solution)/shard_map/pallas_call | solution.py:1151
  388.6 1.5 multiply_reduce_fusion.2
  393.7 67.5 %shard_map.269 = (f32[256,1152]{1,0:T(8,128)}, bf16[4,2,288,864]{3,2,1,0:T(8,128)(2,1)}, bf16[2,864,576]{2,1,0:T(8,128)(2,1)}) custom-call(bf16[256,1152]{1,0:T(8,128)(2,1)} %fusion.own, bf16[2,4,256,1152]{3,2,1,0:T(8,128)(2,1)} %get-tuple-element.168.group, bf16[4,2,288,864]{3,2,1,0:T(8,128)(2,1)} %all-gather.9.cloned.1.call-done.gu_ref, ...), custom_call_target="tpu_custom_call" | custom-call | flops 1 | bytes 1 | tf_op jit(solution)/shard_map/pallas_call | solution.py:1151
  461.8 27.4 %shard_map.270 = (f32[256,1152]{1,0:T(8,128)}, bf16[256,1536]{1,0:T(8,128)(2,1)}, bf16[256,1152]{1,0:T(8,128)(2,1)}, f32[2,2560]{1,0:T(2,128)}, bf16[256,1152]{1,0:T(8,128)(2,1)}, /*index=5*/f32[1,1152]{1,0:T(1,128)}) custom-call(f32[256,1152]{1,0:T(8,128)} %get-tuple-element.170.refs_0_, f32[256,1152]{1,0:T(8,128)} %copy-done.4, ...), custom_call_target="tpu_custom_call" | custom-call | tf_op jit(solution)/shard_map/pallas_call | solution.py:785
  489.2 94.4 %shard_map.271 = (f32[256,1152]{1,0:T(8,128)}, bf16[4,2,288,864]{3,2,1,0:T(8,128)(2,1)}, bf16[2,864,576]{2,1,0:T(8,128)(2,1)}) custom-call(bf16[256,1152]{1,0:T(8,128)(2,1)} %get-tuple-element.176.own, bf16[2,4,256,1152]{3,2,1,0:T(8,128)(2,1)} %get-tuple-element.177.group, bf16[4,2,288,864]{3,2,1,0:T(8,128)(2,1)} %all-gather.5.cloned.1.call-done.gu_ref, ...), custom_call_target="tpu_custom_call" | custom-call | flops 1 | bytes 1 | tf_op jit(solution)/shard_map/pallas_call | solution.py:1151
  583.7 24.3 %shard_map.272 = (f32[256,1152]{1,0:T(8,128)}, bf16[256,1536]{1,0:T(8,128)(2,1)}, bf16[256,1152]{1,0:T(8,128)(2,1)}, f32[2,2560]{1,0:T(2,128)}) custom-call(f32[256,1152]{1,0:T(8,128)} %get-tuple-element.179.refs_0_, f32[256,1152]{1,0:T(8,128)} %get-tuple-element.180.refs_1_, f32[256,1152]{1,0:T(8,128)} %get-tuple-element.181.refs_2_, ...), custom_call_target="tpu_custom_call" | custom-call | tf_op jit(solution)/shard_map/pallas_call | solution.py:785
  608.1 1.4 scatter.30
  612.3 148.0 %shard_map.273 = (f32[144,768]{1,0:T(8,128)}, f32[128,576]{1,0:T(8,128)}, f32[8,256]{1,0:T(8,128)}, f32[432,576]{1,0:T(8,128)}) custom-call(bf16[256,1152]{1,0:T(8,128)(2,1)} %get-tuple-element.148.refs_0_, bf16[256,1536]{1,0:T(8,128)(2,1)} %get-tuple-element.189.refs_1_, bf16[256,1024]{1,0:T(8,128)(2,1)} %get-tuple-element.190.refs_2_, ...), custom_call_target="tpu_custom_call" | custom-call | flops 1 | bytes 1 | tf_op jit(solution)/shard_map/pallas_call | solution.py:506
  760.4 64.4 %shard_map.274 = (f32[2,72,768]{2,1,0:T(8,128)}, f32[2,64,576]{2,1,0:T(8,128)}, f32[2,72,6912]{2,1,0:T(8,128)}, f32[2,432,576]{2,1,0:T(8,128)}, f32[2,72,768]{2,...) custom-call(f32[144,768]{1,0:T(8,128)} %get-tuple-element.202.refs_0_, ...), custom_call_target="tpu_custom_call" | custom-call | tf_op jit(solution)/shard_map/pallas_call | solution.py:1371
  831.9 4.5 copy.85
  836.4 1.4 copy.86
  839.8 2.0 copy.89
  842.9 1.4 copy.90
  (121 shorter events, 24.9 us)
Async XLA Ops:
  7.2 2.3 copy-start.24
  7.2 2.3 copy-start.28
  7.2 177.3 %all-gather.7.cloned.1.call-start = ((), (), s32[]{:S(2)}) async-start(), calls=%async_computation.4 | async-start | bytes 2764800 | tf_op jit(solution)/shard_map/all_gather | solution.py:1471
  9.4 175.1 %all-gather.5.cloned.1.call-start = ((), (), s32[]{:S(2)}) async-start(), calls=%async_computation.3 | async-start | bytes 5160960 | tf_op jit(solution)/shard_map/all_gather | solution.py:1464
  94.1 4.3 copy-start.23
  96.4 190.8 %all-gather.11.cloned.1.call-start = ((), (), s32[]{:S(2)}) async-start(), calls=%async_computation.6 | async-start | bytes 2764800 | tf_op jit(solution)/shard_map/all_gather | solution.py:1471
  101.0 21.5 %copy-start.12 = (bf16[8,144,864]{2,1,0:T(8,128)(2,1)S(1)}, bf16[8,144,864]{2,1,0:T(8,128)(2,1)}, u32[]{:S(2)}) copy-start(bf16[8,144,864]{2,1,0:T(8,128)(2,1)} %get-tuple-element.151) | copy-start | bytes 5971972
  122.4 194.2 %all-gather.9.cloned.1.call-start = ((), (), s32[]{:S(2)}) async-start(), calls=%async_computation.5 | async-start | bytes 5160960 | tf_op jit(solution)/shard_map/all_gather | solution.py:1464
  123.5 488.1 %reduce-scatter.6.cloned.1.call-start = ((), (), s32[]{:S(2)}) async-start(), calls=%async_computation.8 | async-start | bytes 2764800 | tf_op jit(solution)/shard_map/reduce_scatter | solution.py:1543
  182.2 68.9 %copy-start.20 = (f32[2,2560]{1,0:T(2,128)}, f32[2,2560]{1,0:T(2,128)S(1)}, u32[]{:S(2)}) copy-start(f32[2,2560]{1,0:T(2,128)S(1)} %reshape_squeeze.7.refs_5_.refs_10_) | copy-start | bytes 61444
  316.7 73.5 %copy-start.6 = (f32[256,1152]{1,0:T(8,128)S(1)}, f32[256,1152]{1,0:T(8,128)}, u32[]{:S(2)}) copy-start(f32[256,1152]{1,0:T(8,128)} %get-tuple-element.163.refs_7_) | copy-start | bytes 3538948
  316.7 73.5 %copy-start.8 = (bf16[1,256,1152]{2,1,0:T(8,128)(2,1)S(1)}, bf16[1,256,1152]{2,1,0:T(8,128)(2,1)}, u32[]{:S(2)}) copy-start(bf16[1,256,1152]{2,1,0:T(8,128)(2,1)} %param.28) | copy-start | bytes 1769476
  461.2 150.5 %reduce-scatter.4.cloned.1.call-start = ((), (), s32[]{:S(2)}) async-start(), calls=%async_computation.7 | async-start | bytes 5160960 | tf_op jit(solution)/shard_map/reduce_scatter | solution.py:1551
  461.8 298.6 %reduce-scatter.8.cloned.1.call-start = ((), (), s32[]{:S(2)}) async-start(), calls=%async_computation.9 | async-start | bytes 5160960 | tf_op jit(solution)/shard_map/reduce_scatter | solution.py:1551
  583.7 24.4 %copy-start.25 = (f32[1,1152]{1,0:T(1,128)S(1)}, f32[1,1152]{1,0:T(1,128)}, u32[]{:S(2)}) copy-start(f32[1,1152]{1,0:T(1,128)} %get-tuple-element.197) | copy-start | bytes 13828
  583.7 25.8 %copy-start.22 = (f32[2,2560]{1,0:T(2,128)S(1)}, f32[2,2560]{1,0:T(2,128)}, u32[]{:S(2)}) copy-start(f32[2,2560]{1,0:T(2,128)} %get-tuple-element.198) | copy-start | bytes 61444
  760.3 65.7 %copy-start.26 = (f32[2,1,160]{2,1,0:T(1,128)S(1)}, f32[2,1,160]{2,1,0:T(1,128)}, u32[]{:S(2)}) copy-start(f32[2,1,160]{2,1,0:T(1,128)} %param.40) | copy-start | bytes 3844
  760.4 65.7 %copy-start.27 = (f32[2,1,160]{2,1,0:T(1,128)S(1)}, f32[2,1,160]{2,1,0:T(1,128)}, u32[]{:S(2)}) copy-start(f32[2,1,160]{2,1,0:T(1,128)} %param.41) | copy-start | bytes 3844
  760.4 68.8 %copy-start.13 = (f32[256,1152]{1,0:T(8,128)S(1)}, f32[256,1152]{1,0:T(8,128)}, u32[]{:S(2)}) copy-start(f32[256,1152]{1,0:T(8,128)} %get-tuple-element.201) | copy-start | bytes 3538948
  829.2 2.0 copy-start.19
  831.9 4.5 copy-start.11
  836.4 2.1 copy-start.18
  836.4 3.4 copy-start.7
  839.8 3.1 copy-start.10
  (12 other events, 15.0 us)
Sparse Core Ops, SparseCore 0:
  10.2 82.7 all-gather.6
  96.5 79.8 all-gather.4
  178.5 57.4 all-gather.10
  238.1 78.5 all-gather.8
  461.3 58.1 reduce-scatter.5
  521.7 73.3 reduce-scatter.3
  597.5 133.3 reduce-scatter.7

commit v2 on v1

--- a/solution.py
+++ b/solution.py
@@ -113,19 +113,15 @@
     cores, planes, members = sizes
     rest = list(refs)
     take = lambda number: [rest.pop(0) for _ in range(number)]
-    gu, qkv, out, packet = take(4)
-    gu_result, mixed, project, packets, qkv_later, out_later = take(6)
+    qkv, out, packet = take(3)
+    mixed, project, packets, qkv_later, out_later = take(5)
     packet_slots, qkv_slots, out_slots, send_sem, recv_sem = take(5)
-    pieces, gu_send, gu_recv, gu_own, later_send, later_recv = take(6)
+    later_send, later_recv = take(2)
     qkv_low, out_low, later_own = take(3)
     gather = Spread(sizes, [packet_slots, qkv_slots, out_slots], send_sem, recv_sem)
     here = tuple(gather.place[name] for name in EVERY)
-    core, zd, tp = here
-    group = []
-    for step in range(1, cores * members):
-        far = lax.rem(core + step // members, cores), lax.rem(tp + step % members, members)
-        group.append((dict(zip(GROUP, far)), linear(far, (cores, members))))
-    enter(gather.partners() + [device for device, _ in group])
+    zd = gather.place["zd"]
+    enter(gather.partners())
     packet_slots[here] = packet[...]
 
     def place_rows(source, layer, slot, index):
@@ -166,6 +162,24 @@
             own = pltpu.make_async_copy(low.at[layer - 1], target, later_own.at[k, layer])
             own.start()
             moves.append(own)
+    gather.stage("tp")
+    gather.stage("head")
+    gather.finish()
+    side_by_side(sizes, (qkv_slots, out_slots), (mixed, project))
+    packets[...] = packet_slots[...]
+    for copy in moves:
+        copy.wait()
+
+
+def rows_kernel(sizes, gu, gu_result, pieces, gu_send, gu_recv, gu_own):
+    cores, planes, members = sizes
+    core, _, tp = (lax.axis_index(axis) for axis in EVERY)
+    moves = []
+    group = []
+    for step in range(1, cores * members):
+        far = lax.rem(core + step // members, cores), lax.rem(tp + step % members, members)
+        group.append((dict(zip(GROUP, far)), linear(far, (cores, members))))
+    enter([device for device, _ in group])
     layers, rows, columns = gu.shape
     block = columns // (planes * members)
     half = planes // cores
@@ -198,13 +212,30 @@
     own = pltpu.make_async_copy(pieces.at[me], gu_result.at[me], gu_own)
     own.start()
     moves.append(own)
-    gather.stage("tp")
-    gather.stage("head")
-    gather.finish()
-    side_by_side(sizes, (qkv_slots, out_slots), (mixed, project))
-    packets[...] = packet_slots[...]
     for copy in moves:
         copy.wait()
+
+
+def exchanged_rows(w_gu, ident):
+    sizes = tuple(lax.axis_size(axis) for axis in EVERY)
+    cores, _, members = sizes
+    vmem, dma = pltpu.VMEM, pltpu.SemaphoreType.DMA
+    layers, rows, columns = w_gu.shape
+    piece = (
+        cores * members,
+        -(-layers * rows // 16) * 16,
+        columns // (cores * members),
+    )
+    return pl.pallas_call(
+        partial(rows_kernel, sizes),
+        out_shape=jax.ShapeDtypeStruct(piece, bf16),
+        in_specs=[pl.BlockSpec(memory_space=pltpu.VMEM)],
+        out_specs=pl.BlockSpec(memory_space=pl.ANY),
+        scratch_shapes=[vmem(piece, bf16)] + [dma((cores * members - 1,))] * 2 + [dma],
+        compiler_params=pltpu.CompilerParams(
+            collective_id=ident, has_side_effects=True, vmem_limit_bytes=48 * 2**20
+        ),
+    )(w_gu)
 
 
 def side_by_side(sizes, slots, results):
@@ -239,7 +270,7 @@
     return slots, outs
 
 
-def start(w_gu, w_qkv, w_out, packet, ident):
+def start(w_qkv, w_out, packet, ident):
     sizes = tuple(lax.axis_size(axis) for axis in EVERY)
     cores, planes, members = sizes
     vmem, dma = pltpu.VMEM, pltpu.SemaphoreType.DMA
@@ -247,21 +278,15 @@
     shape = jax.ShapeDtypeStruct
     tall = [-(-w.shape[1] // 16) * 16 for w in (w_qkv, w_out)]
     slots, outs = whole_shapes(sizes, tall, (w_qkv, w_out))
-    layers, rows, columns = w_gu.shape
-    piece = (
-        cores * members,
-        -(-layers * rows // 16) * 16,
-        columns // (cores * members),
-    )
+    layers = w_qkv.shape[0]
     later = [
         shape((layers - 1, planes, t, w.shape[2]), bf16) for t, w in zip(tall, (w_qkv, w_out))
     ]
-    operands = [w_gu, w_qkv, w_out, packet]
-    outs = [shape(piece, bf16)] + outs + [shape(sizes + packet.shape, f32)] + later
-    out_specs = [there] + [here] * 3 + [there] * 2
+    operands = [w_qkv, w_out, packet]
+    outs = outs + [shape(sizes + packet.shape, f32)] + later
+    out_specs = [here] * 3 + [there] * 2
     moves = math.prod(sizes) - 1
     scratch = [vmem(sizes + packet.shape, f32)] + slots + [dma((3, moves))] * 2
-    scratch += [vmem(piece, bf16), dma((cores * members - 1,)), dma((cores * members - 1,)), dma]
     scratch += [dma((2, layers, planes))] * 2
     scratch += [
         vmem((layers - 1, t, w.shape[2]), bf16) for t, w in zip(tall, (w_qkv, w_out))
@@ -1448,9 +1473,8 @@
     packet = jnp.zeros((8, lanes), f32)
     packet = packet.at[:LAYERS, :gain_cols].set(norm_gains[:, 0].astype(bf16).astype(f32))
     packet = packet.at[LAYERS, 0].set(jnp.sum(valid_mask.astype(f32)))
-    gu_pieces, w_mixed, w_project, packets, *later = start(
-        w_gu, w_qkv, w_out, packet, 0
-    )
+    gu_pieces, packet = lax.optimization_barrier((exchanged_rows(w_gu, 1), packet))
+    w_mixed, w_project, packets, *later = start(w_qkv, w_out, packet, 0)
     attn_weights = [w_mixed, w_project]
     gu_pieces = gu_pieces[:, : LAYERS * gu_rows].reshape(cores * PLANE, LAYERS, gu_rows, share)
     packets = packets.reshape(cores, seq_devices, 8, lanes)

time: 860 us -> 852 us (level)
  waiting for transfers between devices: 30.2 us -> 0.76 us
  Pallas kernels: 759 us -> 781 us
    all_gather x2, waiting for transfers between devices: 29.5 us -> 0.04 us  [gate_up_rows(): pieces = lax.all_gather(pieces, 'zd', axis=0)]
    pallas_call x0 -> x1, Pallas kernels: none -> 28.3 us  [exchanged_rows(): pl.pallas_call(partial(rows_kernel, sizes), out_shape=jax.ShapeDtypeStruc...]
    pallas_call x2, Pallas kernels: 55.3 us -> 78.5 us  [attn_forward(): pl.pallas_call(partial(attn_forward_kernel, planes, reach, earlier is not...]
    pallas_call x1, Pallas kernels: 82.7 us -> 60.2 us  [start(): pl.pallas_call(partial(start_kernel, sizes), out_shape=outs, in_specs=[he...]
    pallas_call x1, Pallas kernels: 56.6 us -> 47.6 us  [later_weights(): pl.pallas_call(partial(later_kernel, sizes, layer), out_shape=outs, in_sp...]
    pallas_call x2, Pallas kernels: 51.8 us -> 60.7 us  [attn_backward(): pl.pallas_call(partial(attn_backward_kernel, planes, reach, earlier is no...]
  transfers between devices with their start and end apart: 7 -> 7, of which waited for: 1 -> 0; matrix products, arithmetic and copies ran while one was open for 2% -> 2% of each run, Pallas kernels for 65% -> 69%
where the time goes in v2:
time: 852 us; the launch traced here: 845 us
  Pallas kernels  781 us (92%)
  local copies, waits for them, and re-layouts  34.6 us (4%)
  between operations  17.6 us (2%)
  other arithmetic  10.7 us (1%)
    pallas_call x4, Pallas kernels, ffn(): pl.pallas_call(kernel, out_shape=out_shape, in_specs=in_specs, out_specs=...  292 us
    pallas_call x1, Pallas kernels, collect(): pl.pallas_call(partial(collect_kernel, sizes, layers, down is not None),...  149 us
    pallas_call x2, Pallas kernels, attn_forward(): pl.pallas_call(partial(attn_forward_kernel, planes, reach, earlier is not...  78.5 us
    pallas_call x1, Pallas kernels, update(): pl.pallas_call(partial(update_kernel, sizes, [len(g) for g in gradients])...  64.4 us
    pallas_call x2, Pallas kernels, attn_backward(): pl.pallas_call(partial(attn_backward_kernel, planes, reach, earlier is no...  60.7 us
    pallas_call x1, Pallas kernels, start(): pl.pallas_call(partial(start_kernel, sizes), out_shape=outs, in_specs=[he...  60.2 us
    pallas_call x1, Pallas kernels, later_weights(): pl.pallas_call(partial(later_kernel, sizes, layer), out_shape=outs, in_sp...  47.6 us
    pallas_call x1, Pallas kernels, exchanged_rows(): pl.pallas_call(partial(rows_kernel, sizes), out_shape=jax.ShapeDtypeStruc...  28.3 us
  transfers between devices with their start and end apart: 7, of which 0 were waited for; matrix products, arithmetic and copies ran while one was open for 2% of the time, Pallas kernels for 69%

profile of v2, /device:TPU:0, one launch (start us, length us, event | category | flops | bytes accessed | tf_op | source)
XLA Modules:
  0.0 845.0 jit_solution(8489077232107682044)
XLA Ops:
  7.2 2.1 slice.176
  9.4 2.1 copy-done
  11.5 28.3 %shard_map.263 = bf16[8,144,864]{2,1,0:T(8,128)(2,1)S(1)} custom-call(f32[2,72,6912]{2,1,0:T(8,128)S(1)} %copy-done), custom_call_target="tpu_custom_call" | custom-call | tf_op jit(solution)/shard_map/pallas_call | solution.py:229
  42.3 60.2 %shard_map.264 = (bf16[1152,1536]{1,0:T(8,128)(2,1)}, bf16[1024,1152]{1,0:T(8,128)(2,1)}, f32[2,4,4,8,256]{4,3,2,1,0:T(8,128)}, bf16[1,4,80,768]{3,2,1,0:T(8,128)(2,1)}, bf16[1,4,64,576]{3,2,1,0:T(8,128)(2,1)}) custom-call(f32[2,72,768]{2,1,0:T(8,128)} %refs_10_.1, f32[2,64,576]{2,1,0:T(8,128)} %refs_11_.1, f32[8,256]{1,0:T(8,128)} %copy-done.21), custom_call_target="tpu_custom_call" | custom-call | tf_op jit(solution)/shard_map/pallas_call | solution.py:294
  107.1 32.4 %shard_map.265 = (f32[256,1152]{1,0:T(8,128)}, bf16[256,1152]{1,0:T(8,128)(2,1)}, f32[256,1536]{1,0:T(8,128)}, bf16[256,1024]{1,0:T(8,128)(2,1)}, bf16[1,768,512...) custom-call(bf16[256,1152]{1,0:T(8,128)(2,1)} %bitcast.55, ...), custom_call_target="tpu_custom_call" | custom-call | tf_op jit(solution)/shard_map/pallas_call | solution.py:667
  139.5 2.1 slice.175
  143.3 47.6 %shard_map.266 = (bf16[1152,1536]{1,0:T(8,128)(2,1)}, bf16[1024,1152]{1,0:T(8,128)(2,1)S(1)}) custom-call(bf16[1,4,80,768]{3,2,1,0:T(8,128)(2,1)S(1)} %copy-done.2, bf16[1,4,64,576]{3,2,1,0:T(8,128)(2,1)S(1)} %copy-done.3), custom_call_target="tpu_custom_call" | custom-call | tf_op jit(solution)/shard_map/pallas_call | solution.py:311
  191.0 1.4 copy-done.1
  192.5 1.5 slice_reduce_fusion.2
  194.8 65.2 %shard_map.267 = (bf16[2,4,256,1152]{3,2,1,0:T(8,128)(2,1)}, bf16[864,1152]{1,0:T(8,128)(2,1)}, f32[256,1152]{1,0:T(8,128)}) custom-call(bf16[256,1152]{1,0:T(8,128)(2,1)} %get-tuple-element.161.own, bf16[4,2,288,864]{3,2,1,0:T(8,128)(2,1)} %all-gather.5.cloned.1.call-done.gu_ref, bf16[1,1728,576]{2,1,0:T(8,128)(2,1)} %all-gather.7.cloned.1.call-done.halves_ref), custom_call_target="tpu_custom_call" | custom-call | flops 1 | bytes 1 | tf_op jit(solution)/shard_map/pallas_call | solution.py:1176
  260.0 46.2 %shard_map.268 = (f32[256,1152]{1,0:T(8,128)}, bf16[256,1152]{1,0:T(8,128)(2,1)}, f32[256,1536]{1,0:T(8,128)}, bf16[256,1024]{1,0:T(8,128)(2,1)}, bf16[1,768,512...) custom-call(f32[256,1152]{1,0:T(8,128)} %get-tuple-element.151.refs_, ...), custom_call_target="tpu_custom_call" | custom-call | tf_op jit(solution)/shard_map/pallas_call | solution.py:667
  306.3 69.6 %shard_map.269 = (bf16[2,4,256,1152]{3,2,1,0:T(8,128)(2,1)}, bf16[864,1152]{1,0:T(8,128)(2,1)}, f32[256,1152]{1,0:T(8,128)}) custom-call(bf16[256,1152]{1,0:T(8,128)(2,1)} %get-tuple-element.166.own, bf16[4,2,288,864]{3,2,1,0:T(8,128)(2,1)} %all-gather.9.cloned.1.call-done.gu_ref, bf16[1,1728,576]{2,1,0:T(8,128)(2,1)} %all-gather.11.cloned.1.call-done.halves_ref), custom_call_target="tpu_custom_call" | custom-call | flops 1 | bytes 1 | tf_op jit(solution)/shard_map/pallas_call | solution.py:1176
  375.9 1.5 multiply_reduce_fusion.2
  380.9 67.5 %shard_map.270 = (f32[256,1152]{1,0:T(8,128)}, bf16[4,2,288,864]{3,2,1,0:T(8,128)(2,1)}, bf16[2,864,576]{2,1,0:T(8,128)(2,1)}) custom-call(bf16[256,1152]{1,0:T(8,128)(2,1)} %fusion.own, bf16[2,4,256,1152]{3,2,1,0:T(8,128)(2,1)} %get-tuple-element.170.group, bf16[4,2,288,864]{3,2,1,0:T(8,128)(2,1)} %all-gather.9.cloned.1.call-done.gu_ref, ...), custom_call_target="tpu_custom_call" | custom-call | flops 1 | bytes 1 | tf_op jit(solution)/shard_map/pallas_call | solution.py:1176
  449.1 32.4 %shard_map.271 = (f32[256,1152]{1,0:T(8,128)}, bf16[256,1536]{1,0:T(8,128)(2,1)}, bf16[256,1152]{1,0:T(8,128)(2,1)}, f32[2,2560]{1,0:T(2,128)}, bf16[256,1152]{1,0:T(8,128)(2,1)}, /*index=5*/f32[1,1152]{1,0:T(1,128)}) custom-call(f32[256,1152]{1,0:T(8,128)} %get-tuple-element.172.refs_0_, f32[256,1152]{1,0:T(8,128)} %copy-done.5, ...), custom_call_target="tpu_custom_call" | custom-call | tf_op jit(solution)/shard_map/pallas_call | solution.py:810
  481.5 89.7 %shard_map.272 = (f32[256,1152]{1,0:T(8,128)}, bf16[4,2,288,864]{3,2,1,0:T(8,128)(2,1)}, bf16[2,864,576]{2,1,0:T(8,128)(2,1)}) custom-call(bf16[256,1152]{1,0:T(8,128)(2,1)} %get-tuple-element.178.own, bf16[2,4,256,1152]{3,2,1,0:T(8,128)(2,1)} %get-tuple-element.179.group, bf16[4,2,288,864]{3,2,1,0:T(8,128)(2,1)} %all-gather.5.cloned.1.call-done.gu_ref, ...), custom_call_target="tpu_custom_call" | custom-call | flops 1 | bytes 1 | tf_op jit(solution)/shard_map/pallas_call | solution.py:1176
  571.2 28.3 %shard_map.273 = (f32[256,1152]{1,0:T(8,128)}, bf16[256,1536]{1,0:T(8,128)(2,1)}, bf16[256,1152]{1,0:T(8,128)(2,1)}, f32[2,2560]{1,0:T(2,128)}) custom-call(f32[256,1152]{1,0:T(8,128)} %get-tuple-element.181.refs_0_, f32[256,1152]{1,0:T(8,128)} %get-tuple-element.182.refs_1_, f32[256,1152]{1,0:T(8,128)} %get-tuple-element.183.refs_2_, ...), custom_call_target="tpu_custom_call" | custom-call | tf_op jit(solution)/shard_map/pallas_call | solution.py:810
  599.6 1.4 scatter.30
  603.8 148.8 %shard_map.274 = (f32[144,768]{1,0:T(8,128)}, f32[128,576]{1,0:T(8,128)}, f32[8,256]{1,0:T(8,128)}, f32[432,576]{1,0:T(8,128)}) custom-call(bf16[256,1152]{1,0:T(8,128)(2,1)} %get-tuple-element.150.refs_0_, bf16[256,1536]{1,0:T(8,128)(2,1)} %get-tuple-element.191.refs_1_, bf16[256,1024]{1,0:T(8,128)(2,1)} %get-tuple-element.192.refs_2_, ...), custom_call_target="tpu_custom_call" | custom-call | flops 1 | bytes 1 | tf_op jit(solution)/shard_map/pallas_call | solution.py:531
  752.7 64.4 %shard_map.275 = (f32[2,72,768]{2,1,0:T(8,128)}, f32[2,64,576]{2,1,0:T(8,128)}, f32[2,72,6912]{2,1,0:T(8,128)}, f32[2,432,576]{2,1,0:T(8,128)}, f32[2,72,768]{2,...) custom-call(f32[144,768]{1,0:T(8,128)} %get-tuple-element.204.refs_0_, ...), custom_call_target="tpu_custom_call" | custom-call | tf_op jit(solution)/shard_map/pallas_call | solution.py:1396
  824.3 4.5 copy.85
  828.7 1.4 copy.86
  832.2 2.0 copy.89
  835.2 1.4 copy.90
  (122 shorter events, 25.4 us)
Async XLA Ops:
  7.2 187.6 %all-gather.7.cloned.1.call-start = ((), (), s32[]{:S(2)}) async-start(), calls=%async_computation.4 | async-start | bytes 2764800 | tf_op jit(solution)/shard_map/all_gather | solution.py:1495
  9.4 185.4 %all-gather.5.cloned.1.call-start = ((), (), s32[]{:S(2)}) async-start(), calls=%async_computation.3 | async-start | bytes 5160960 | tf_op jit(solution)/shard_map/all_gather | solution.py:1488
  9.4 2.1 copy-start
  11.5 28.3 %copy-start.24 = (f32[2,1,160]{2,1,0:T(1,128)S(1)}, f32[2,1,160]{2,1,0:T(1,128)}, u32[]{:S(2)}) copy-start(f32[2,1,160]{2,1,0:T(1,128)} %param.35) | copy-start | bytes 3844
  11.5 28.3 %copy-start.28 = (s32[1,256]{1,0:T(1,128)S(1)}, s32[1,256]{1,0:T(1,128)}, u32[]{:S(2)}) copy-start(s32[1,256]{1,0:T(1,128)} %param.30) | copy-start | bytes 3076
  42.2 62.2 %copy-start.23 = (s32[2,4096]{1,0:T(2,128)S(1)}, s32[2,4096]{1,0:T(2,128)}, u32[]{:S(2)}) copy-start(s32[2,4096]{1,0:T(2,128)} %param.29) | copy-start | bytes 98308
  42.3 263.9 %all-gather.11.cloned.1.call-start = ((), (), s32[]{:S(2)}) async-start(), calls=%async_computation.6 | async-start | bytes 2764800 | tf_op jit(solution)/shard_map/all_gather | solution.py:1495
  141.7 164.6 %all-gather.9.cloned.1.call-start = ((), (), s32[]{:S(2)}) async-start(), calls=%async_computation.5 | async-start | bytes 5160960 | tf_op jit(solution)/shard_map/all_gather | solution.py:1488
  142.8 460.4 %reduce-scatter.6.cloned.1.call-start = ((), (), s32[]{:S(2)}) async-start(), calls=%async_computation.8 | async-start | bytes 2764800 | tf_op jit(solution)/shard_map/reduce_scatter | solution.py:1567
  192.4 67.6 %copy-start.20 = (f32[2,2560]{1,0:T(2,128)}, f32[2,2560]{1,0:T(2,128)S(1)}, u32[]{:S(2)}) copy-start(f32[2,2560]{1,0:T(2,128)S(1)} %reshape_squeeze.7.refs_5_.refs_10_) | copy-start | bytes 61444
  306.3 71.1 %copy-start.7 = (f32[256,1152]{1,0:T(8,128)S(1)}, f32[256,1152]{1,0:T(8,128)}, u32[]{:S(2)}) copy-start(f32[256,1152]{1,0:T(8,128)} %get-tuple-element.165.refs_7_) | copy-start | bytes 3538948
  306.3 71.1 %copy-start.9 = (bf16[1,256,1152]{2,1,0:T(8,128)(2,1)S(1)}, bf16[1,256,1152]{2,1,0:T(8,128)(2,1)}, u32[]{:S(2)}) copy-start(bf16[1,256,1152]{2,1,0:T(8,128)(2,1)} %param.28) | copy-start | bytes 1769476
  448.5 154.7 %reduce-scatter.4.cloned.1.call-start = ((), (), s32[]{:S(2)}) async-start(), calls=%async_computation.7 | async-start | bytes 5160960 | tf_op jit(solution)/shard_map/reduce_scatter | solution.py:1575
  449.0 303.7 %reduce-scatter.8.cloned.1.call-start = ((), (), s32[]{:S(2)}) async-start(), calls=%async_computation.9 | async-start | bytes 5160960 | tf_op jit(solution)/shard_map/reduce_scatter | solution.py:1575
  571.2 28.4 %copy-start.25 = (f32[1,1152]{1,0:T(1,128)S(1)}, f32[1,1152]{1,0:T(1,128)}, u32[]{:S(2)}) copy-start(f32[1,1152]{1,0:T(1,128)} %get-tuple-element.199) | copy-start | bytes 13828
  571.2 29.8 %copy-start.22 = (f32[2,2560]{1,0:T(2,128)S(1)}, f32[2,2560]{1,0:T(2,128)}, u32[]{:S(2)}) copy-start(f32[2,2560]{1,0:T(2,128)} %get-tuple-element.200) | copy-start | bytes 61444
  752.7 65.7 %copy-start.26 = (f32[2,1,160]{2,1,0:T(1,128)S(1)}, f32[2,1,160]{2,1,0:T(1,128)}, u32[]{:S(2)}) copy-start(f32[2,1,160]{2,1,0:T(1,128)} %param.40) | copy-start | bytes 3844
  752.7 65.7 %copy-start.27 = (f32[2,1,160]{2,1,0:T(1,128)S(1)}, f32[2,1,160]{2,1,0:T(1,128)}, u32[]{:S(2)}) copy-start(f32[2,1,160]{2,1,0:T(1,128)} %param.41) | copy-start | bytes 3844
  752.7 68.8 %copy-start.13 = (f32[256,1152]{1,0:T(8,128)S(1)}, f32[256,1152]{1,0:T(8,128)}, u32[]{:S(2)}) copy-start(f32[256,1152]{1,0:T(8,128)} %get-tuple-element.203) | copy-start | bytes 3538948
  821.5 2.0 copy-start.19
  824.3 4.5 copy-start.12
  828.7 2.1 copy-start.18
  828.7 3.4 copy-start.8
  832.2 3.1 copy-start.11
  (12 other events, 15.5 us)
Sparse Core Ops, SparseCore 0:
  10.2 70.7 all-gather.6
  83.1 80.2 all-gather.4
  165.6 57.7 all-gather.10
  225.4 78.5 all-gather.8
  448.6 63.1 reduce-scatter.5
  513.9 73.3 reduce-scatter.3
  589.8 131.3 reduce-scatter.7
